TPU v7x, 32 devices: a whole 2x2x4 slice. The times are simulated.
32 devices in a mesh: groups: 2 (over y), dom: 4 (over z), batch: 2 (over x), sub: 2 (over core).
Axes of the slice: x: 2, y: 2, z: 4, core: 2. Of those that a mesh axis runs over, the one named last changes fastest.
Arguments:
- solution: float32 [32768], P(('groups', 'dom', 'batch', 'sub')), parts along dimension 0, may hold values from -6 to 6
- residual: float32 [32768], P(('groups', 'dom', 'batch', 'sub')), parts along dimension 0, may hold values from -18 to 18
- direction: float32 [32768], P(('groups', 'dom', 'batch', 'sub')), parts along dimension 0, may hold values from -18 to 18
- inverse_diagonal: float32 [32768], P(('groups', 'dom', 'batch', 'sub')), parts along dimension 0, may hold values from 0.25 to 2
- schur_blocks: float32 [96, 602, 602], P(('groups', 'dom', 'batch', 'sub')), parts along dimension 0, may hold values from -1 to 4, as said below
- elem_dofs: int32 [96, 602], P(('groups', 'dom', 'batch', 'sub')), parts along dimension 0, may hold values from 0 to 4095, as said below
- element_order: int32 [96], P(('groups', 'dom', 'batch', 'sub')), parts along dimension 0, may hold values from 4 to 10
- left_slots: int32 [32, 256], P(('groups', 'dom', 'batch', 'sub')), parts along dimension 0, may hold values from 0 to 1023, as said below
- right_slots: int32 [32, 256], P(('groups', 'dom', 'batch', 'sub')), parts along dimension 0, may hold values from 0 to 1023, as said below
- share_count: int32 [32, 2], P(('groups', 'dom', 'batch', 'sub')), parts along dimension 0, may hold values from 0 to 256, as said below
Outputs:
- new_solution: float32 [32768], P(('groups', 'dom', 'batch', 'sub')), parts along dimension 0
- new_residual: float32 [32768], P(('groups', 'dom', 'batch', 'sub')), parts along dimension 0
- new_direction: float32 [32768], P(('groups', 'dom', 'batch', 'sub')), parts along dimension 0
There are 2 independent parts, one for each index of `groups`. A program takes and returns all parts, laid end to end along the dimension named above; each array names one. Nothing has to cross between parts.
Inputs may be any that keep to these rules, and one draw needn't show every extreme that they name: The slots of left_slots[c] and right_slots[c] are all distinct. `right_slots`: distinct from left_slots of the same piece and among themselves. share_count[c, 1] equals share_count[c + 4, 0]; the first partition's left counts and the last partition's right counts are 0; 256 is reached in every draw. `elem_dofs`: every slot named by an element of piece c lies in piece c, or in the piece just before or just after it within the same partition, counted cyclically over the partition's 2 * 2 pieces. `schur_blocks`: symmetric positive definite blocks.
All inputs are finite; a program needn't handle non-finite values.
Results may differ from a plain program's by a relative error of at most 0.000064.
Values sent between devices are 32-bit elements; how exact they have to be, the bound alone decides.
No kernel may reach another device: no remote copies, remote signals or barrier semaphores. Data moves between devices by JAX's collectives and lax.ppermute only.
A program may use at most 64 MiB of HBM per device.

v0:
```python
import jax
import jax.numpy as jnp
from jax import lax
from jax.sharding import PartitionSpec as P

ORDER = 10


def padded(array, sides, width):
    for axis, dim in sides:
        count, length = (lax.axis_size(axis), array.shape[dim])
        up = [(i, (i + 1) % count) for i in range(count)]
        down = [(j, i) for i, j in up]
        last = lax.slice_in_dim(array, length - width, length, axis=dim)
        initial = lax.slice_in_dim(array, 0, width, axis=dim)
        before = lax.ppermute(last, axis, up)
        after = lax.ppermute(initial, axis, down)
        array = jnp.concatenate([before, array, after], axis=dim)
    return array


def shifted(block, axis, distance):
    devices = range(lax.axis_size(axis))
    route = [((i - distance) % len(devices), i) for i in devices]
    return lax.ppermute(block, axis, route)


def passed_along(value, axis, steps):
    count = lax.axis_size(axis)
    initial, last = (max(0, -steps), min(count, count - steps))
    return lax.ppermute(value, axis, [(source, source + steps) for source in range(initial, last)])


def local(
    solution,
    residual,
    direction,
    inverse_diagonal,
    schur_blocks,
    elem_dofs,
    element_order,
    left_slots,
    right_slots,
    share_count,
):
    piece_len = residual.shape[0]
    block_size = schur_blocks.shape[1]
    group_count = lax.axis_size(("batch", "sub"))
    local_len = piece_len * group_count
    live_count = block_size * (6 * element_order * element_order + 2) // (6 * ORDER * ORDER + 2)
    active = jnp.arange(block_size, dtype=jnp.int32)[None, :] < live_count[:, None]
    my_index = lax.axis_index(("batch", "sub"))
    window_start = (my_index + group_count - 1) % group_count * piece_len
    relative = (elem_dofs - window_start + local_len) % local_len
    window = padded(direction, ((("batch", "sub"), 0),), piece_len)
    element_in = jnp.take(window, relative, axis=0)
    element_in = jnp.where(active, element_in, 0.0)
    element_out = jnp.einsum(
        "eij,ej->ei", schur_blocks, element_in, precision=lax.Precision.HIGHEST
    )
    element_out = jnp.where(active, element_out, 0.0)
    window_sum = (
        jnp.zeros((3 * piece_len,), jnp.float32)
        .at[relative.reshape(-1)]
        .add(element_out.reshape(-1))
    )
    from_next = shifted(window_sum[:piece_len], ("batch", "sub"), -1)
    from_prev = shifted(window_sum[2 * piece_len :], ("batch", "sub"), 1)
    own_rows = window_sum[piece_len : 2 * piece_len] + from_next + from_prev
    pair_index = jnp.arange(left_slots.shape[1], dtype=jnp.int32)
    left_active = pair_index < share_count[0, 0]
    right_active = pair_index < share_count[0, 1]
    forward = jnp.where(right_active, own_rows[right_slots[0]], 0.0)
    backward = jnp.where(left_active, own_rows[left_slots[0]], 0.0)
    from_left = passed_along(forward, "dom", 1)
    from_right = passed_along(backward, "dom", -1)
    applied = own_rows.at[left_slots[0]].add(jnp.where(left_active, from_left, 0.0))
    applied = applied.at[right_slots[0]].add(jnp.where(right_active, from_right, 0.0))
    owner_mask = (
        jnp.ones((piece_len,), jnp.float32).at[left_slots[0]].set(jnp.where(left_active, 0.0, 1.0))
    )
    weighted = owner_mask * residual
    old_norm, curvature = lax.psum(
        (
            jnp.sum(weighted * inverse_diagonal * residual),
            jnp.sum(owner_mask * direction * applied),
        ),
        ("dom", "batch", "sub"),
    )
    step_size = old_norm / curvature
    new_solution = solution + step_size * direction
    new_residual = residual - step_size * applied
    precond = inverse_diagonal * new_residual
    new_norm = lax.psum(jnp.sum(owner_mask * new_residual * precond), ("dom", "batch", "sub"))
    new_direction = precond + new_norm / old_norm * direction
    return (new_solution, new_residual, new_direction)


def solution(mesh):
    return jax.shard_map(
        local,
        mesh=mesh,
        in_specs=(
            P(("groups", "dom", "batch", "sub")),
            P(("groups", "dom", "batch", "sub")),
            P(("groups", "dom", "batch", "sub")),
            P(("groups", "dom", "batch", "sub")),
            P(("groups", "dom", "batch", "sub"), None, None),
            P(("groups", "dom", "batch", "sub"), None),
            P(("groups", "dom", "batch", "sub")),
            P(("groups", "dom", "batch", "sub"), None),
            P(("groups", "dom", "batch", "sub"), None),
            P(("groups", "dom", "batch", "sub"), None),
        ),
        out_specs=(
            P(("groups", "dom", "batch", "sub")),
            P(("groups", "dom", "batch", "sub")),
            P(("groups", "dom", "batch", "sub")),
        ),
        check_vma=False,
    )
```

profile of v0, /device:TPU:0, one launch (start us, length us, event | category | flops | bytes accessed | tf_op | source)
XLA Modules:
  0.0 125.8 jit_solution(7006756914638196981)
XLA Ops:
  0.6 0.5 collective-permute-start
  1.1 2.0 %collective-permute-start.1 = (f32[1024]{0:T(1024)}, f32[1024]{0:T(1024)S(1)}, u32[]{:S(2)}, u32[]{:S(2)}) collective-permute-start(f32[1024]{0:T(1024)} %param.12), channel_id=1, source_target_pairs={{1,0},{2,1},{3,2},{0,3},{5,4},{6,5},{7,6},{4,7},{9,8},{10,9},{11,1... | collective-permute-start | bytes 12296 | tf_op jit(solution)/shard_map/ppermute | solution.py:17
  3.1 0.7 compare_select_fusion.1
  3.8 0.1 reshape.106
  3.9 0.7 and_select_fusion
  4.6 0.1 reshape.102
  4.7 0.7 compare_select_fusion.2
  5.4 1.3 %fusion.17 = (s32[1,1]{1,0:T(1,128)}, s32[1,1]{1,0:T(1,128)}) fusion(s32[1,2]{1,0:T(1,128)} %param.19), kind=kLoop, calls=%fused_computation.49 | loop fusion | bytes 16 | tf_op jit(solution)/shard_map/slice | solution.py:71
  6.7 0.7 compare_select_fusion.3
  7.4 0.0 collective-permute-done
  7.4 0.0 collective-permute-done.1
  7.4 0.7 pad_maximum_fusion
  8.1 10.1 %gather_fusion = f32[1806]{0:T(1024)S(1)} fusion(f32[3072]{0:T(1024)S(1)} %pad_maximum_fusion, s32[2048]{0:T(1024)S(1)} %pad_clamp_fusion), kind=kCustom, calls=%fused_computation | custom fusion | bytes 21672 | tf_op jit(solution)/shard_map/jit(_take)/gather | solution.py:56
  18.2 0.1 reshape.105
  18.3 0.1 select_bitcast_fusion
  18.4 0.0 copy-start
  18.4 0.0 copy-start.2
  18.4 6.3 %fusion.2 = f32[3,1,602]{2,1,0:T(1,128)S(1)} fusion(f32[3,602,602]{2,1,0:T(8,128)} %param.14, f32[3,602,1]{1,0,2:T(4,128)S(1)} %select_bitcast_fusion), kind=kOutput, calls=%fused_computation.19 | convolution fusion | flops 13046544 | bytes 4363296 | tf_op jit(solution)/shard_map/eij,ej->ei/dot_general | solution.py:58
  24.7 0.1 bitcast_select_fusion
  24.8 0.1 reshape.140
  24.9 12.2 %scatter_custom_fusion.1 = f32[3072]{0:T(1024)S(1)} fusion(s32[1806]{0:T(1024)S(1)} %fusion.1, f32[1806]{0:T(1024)S(1)} %reshape.140, f32[]{:T(128)} %constant.66.clone.1), kind=kCustom, calls=%fused_computation.21 | custom fusion | flops 1806 | bytes 12292 | tf_op jit(solution)/shard_map/scatter-add | solution.py:65
  37.1 0.7 collective-permute-start.2
  37.9 0.0 collective-permute-start.3
  37.9 0.6 fusion.13
  38.5 1.4 %scatter_custom_fusion = f32[1024]{0:T(1024)S(1)} fusion(s32[256]{0:T(256)S(1)} %bitcast.16, f32[256]{0:T(256)S(1)} %fusion.13, f32[]{:T(128)} %constant.37.clone.1), kind=kCustom, calls=%fused_computation.35 | custom fusion | bytes 4100 | tf_op jit(solution)/shard_map/scatter | solution.py:80
  39.9 0.0 collective-permute-done.2
  39.9 1.0 collective-permute-done.3
  41.0 1.4 %gather_fusion.1 = f32[256]{0:T(256)S(1)} fusion(f32[1024]{0:T(1024)S(1)} %fusion.6, s32[1024]{0:T(1024)S(1)} %pad_clamp_fusion.2), kind=kCustom, calls=%fused_computation.1 | custom fusion | bytes 3072 | tf_op jit(solution)/shard_map/gather | solution.py:73
  42.3 0.7 fusion.10
  43.0 3.6 %collective-permute-start.4 = (f32[256]{0:T(256)S(1)}, f32[256]{0:T(256)S(1)}, u32[]{:S(2)}, u32[]{:S(2)}) collective-permute-start(f32[256]{0:T(256)S(1)} %fusion.10), channel_id=1, source_target_pairs={{0,4},{4,8},{8,12},{1,5},{5,9},{9,13},{2,6},{6,10},{10,14},{3,7},{... | collective-permute-start | bytes 3080 | tf_op jit(solution)/shard_map/ppermute | solution.py:31
  46.6 1.4 %gather_fusion.2 = f32[256]{0:T(256)S(1)} fusion(f32[1024]{0:T(1024)S(1)} %fusion.6, s32[1024]{0:T(1024)S(1)} %pad_clamp_fusion.1), kind=kCustom, calls=%fused_computation.2 | custom fusion | bytes 3072 | tf_op jit(solution)/shard_map/gather | solution.py:74
  48.0 0.7 fusion.11
  48.6 1.3 %collective-permute-start.5 = (f32[256]{0:T(256)S(1)}, f32[256]{0:T(256)S(1)}, u32[]{:S(2)}, u32[]{:S(2)}) collective-permute-start(f32[256]{0:T(256)S(1)} %fusion.11), channel_id=1, source_target_pairs={{4,0},{8,4},{12,8},{5,1},{9,5},{13,9},{6,2},{10,6},{14,10},{7,3},{... | collective-permute-start | bytes 3080 | tf_op jit(solution)/shard_map/ppermute | solution.py:31
  49.9 0.0 collective-permute-done.4
  49.9 0.7 fusion.12
  50.6 2.3 %scatter_fusion = f32[1024]{0:T(1024)S(1)} fusion(f32[1024]{0:T(1024)S(1)} %fusion.6, s32[256]{0:T(256)S(1)} %bitcast.17, f32[256]{0:T(256)S(1)} %fusion.12), kind=kCustom, calls=%fused_computation.5 | custom fusion | flops 256 | bytes 4096 | tf_op jit(solution)/shard_map/scatter-add | solution.py:77
  52.9 1.2 collective-permute-done.5
  54.1 0.6 fusion.9
  54.7 2.3 %scatter_fusion.1 = f32[1024]{0:T(1024)S(1)} fusion(f32[1024]{0:T(1024)S(1)} %scatter_fusion, s32[256]{0:T(256)S(1)} %bitcast.14, f32[256]{0:T(256)S(1)} %fusion.9), kind=kCustom, calls=%fused_computation.6 | custom fusion | flops 256 | bytes 4096 | tf_op jit(solution)/shard_map/scatter-add | solution.py:78
  57.1 0.0 copy-done
  57.1 0.0 copy-done.1
  57.1 0.0 copy-done.2
  57.1 0.6 multiply_reduce_fusion.1
  57.7 33.5 %all-reduce = (f32[]{:T(128)}, f32[]{:T(128)}) all-reduce(f32[]{:T(128)} %get-tuple-element.4, f32[]{:T(128)} %get-tuple-element.3), channel_id=1, replica_groups=mesh['groups'=2,'dom'=4,'batch'=2,'sub'=2] {'dom','batch','sub'}, use_global_device_ids=true, to_apply=%region_2.3 | all-reduce | flops 2 | bytes 16 | tf_op jit(solution)/shard_map/psum | solution.py:83
  92.6 1.2 multiply_reduce_fusion
  93.8 30.1 %psum.23 = f32[]{:T(128)} all-reduce(f32[]{:T(128)} %get-tuple-element.7), channel_id=1, replica_groups=mesh['groups'=2,'dom'=4,'batch'=2,'sub'=2] {'dom','batch','sub'}, use_global_device_ids=true, to_apply=%region_9.10 | all-reduce | flops 1 | bytes 8 | tf_op jit(solution)/shard_map/psum | solution.py:94
  125.2 0.0 copy-done.3
  125.2 0.6 multiply_add_fusion
  (8 shorter events, 0.1 us)
Async XLA Ops:
  0.6 6.8 %collective-permute-start = (f32[1024]{0:T(1024)}, f32[1024]{0:T(1024)S(1)}, u32[]{:S(2)}, u32[]{:S(2)}) collective-permute-start(f32[1024]{0:T(1024)} %param.12), channel_id=1, source_target_pairs={{0,1},{1,2},{2,3},{3,0},{4,5},{5,6},{6,7},{7,4},{8,9},{9,10},{10,1... | collective-permute-start | bytes 12296 | tf_op jit(solution)/shard_map/ppermute | solution.py:16
  1.1 6.3 %collective-permute-start.1 = (f32[1024]{0:T(1024)}, f32[1024]{0:T(1024)S(1)}, u32[]{:S(2)}, u32[]{:S(2)}) collective-permute-start(f32[1024]{0:T(1024)} %param.12), channel_id=1, source_target_pairs={{1,0},{2,1},{3,2},{0,3},{5,4},{6,5},{7,6},{4,7},{9,8},{10,9},{11,1... | collective-permute-start | bytes 12296 | tf_op jit(solution)/shard_map/ppermute | solution.py:17
  18.4 38.7 %copy-start = (f32[1024]{0:T(1024)S(1)}, f32[1024]{0:T(1024)}, u32[]{:S(2)}) copy-start(f32[1024]{0:T(1024)} %param.12) | copy-start | bytes 12292
  18.4 38.7 %copy-start.1 = (f32[1024]{0:T(1024)S(1)}, f32[1024]{0:T(1024)}, u32[]{:S(2)}) copy-start(f32[1024]{0:T(1024)} %param.13) | copy-start | bytes 12292
  18.4 38.7 %copy-start.2 = (f32[1024]{0:T(1024)S(1)}, f32[1024]{0:T(1024)}, u32[]{:S(2)}) copy-start(f32[1024]{0:T(1024)} %param.11) | copy-start | bytes 12292
  18.4 106.8 %copy-start.3 = (f32[1024]{0:T(1024)S(1)}, f32[1024]{0:T(1024)}, u32[]{:S(2)}) copy-start(f32[1024]{0:T(1024)} %param.10) | copy-start | bytes 12292
  37.1 2.8 %collective-permute-start.2 = (f32[1024]{0:T(1024)S(1)}, f32[1024]{0:T(1024)S(1)}, u32[]{:S(2)}, u32[]{:S(2)}) collective-permute-start(f32[1024]{0:T(1024)S(1)} %get-tuple-element.12), channel_id=1, source_target_pairs={{1,0},{2,1},{3,2},{0,3},{5,4},{6,5},{7,6},{4,7},{9,8},{10,9},{11,1... | collective-permute-start | bytes 12296 | tf_op jit(solution)/shard_map/ppermute | solution.py:25
  37.9 3.1 %collective-permute-start.3 = (f32[1024]{0:T(1024)S(1)}, f32[1024]{0:T(1024)S(1)}, u32[]{:S(2)}, u32[]{:S(2)}) collective-permute-start(f32[1024]{0:T(1024)S(1)} %get-tuple-element.13), channel_id=1, source_target_pairs={{3,0},{0,1},{1,2},{2,3},{7,4},{4,5},{5,6},{6,7},{11,8},{8,9},{9,10... | collective-permute-start | bytes 12296 | tf_op jit(solution)/shard_map/ppermute | solution.py:25
  43.0 6.9 %collective-permute-start.4 = (f32[256]{0:T(256)S(1)}, f32[256]{0:T(256)S(1)}, u32[]{:S(2)}, u32[]{:S(2)}) collective-permute-start(f32[256]{0:T(256)S(1)} %fusion.10), channel_id=1, source_target_pairs={{0,4},{4,8},{8,12},{1,5},{5,9},{9,13},{2,6},{6,10},{10,14},{3,7},{... | collective-permute-start | bytes 3080 | tf_op jit(solution)/shard_map/ppermute | solution.py:31
  48.6 5.5 %collective-permute-start.5 = (f32[256]{0:T(256)S(1)}, f32[256]{0:T(256)S(1)}, u32[]{:S(2)}, u32[]{:S(2)}) collective-permute-start(f32[256]{0:T(256)S(1)} %fusion.11), channel_id=1, source_target_pairs={{4,0},{8,4},{12,8},{5,1},{9,5},{13,9},{6,2},{10,6},{14,10},{7,3},{... | collective-permute-start | bytes 3080 | tf_op jit(solution)/shard_map/ppermute | solution.py:31
where the time goes:
time: 126 us
  blocking collectives  63.6 us (50%)
  other arithmetic  26.2 us (21%)
  local copies, waits for them, and re-layouts  15.9 us (13%)
  starting transfers between devices  8.12 us (6%)
  matrix products  6.32 us (5%)
  between operations  3.5 us (3%)
  waiting for transfers between devices  2.19 us (2%)
    psum x1, blocking collectives, local(): lax.psum((jnp.sum(weighted * inverse_diagonal * residual), jnp.sum(owner_...  33.5 us
    psum x1, blocking collectives, local(): lax.psum(jnp.sum(owner_mask * new_residual * precond), ('dom', 'batch', '...  30.1 us
    scatter-add x1, other arithmetic, local(): window_sum = jnp.zeros((3 * piece_len,), jnp.float32).at[relative.reshape...  12.2 us
    gather x2, local copies, waits for them, and re-layouts, local(): element_in = jnp.take(window, relative, axis=0)  10.2 us
    dot_general x1, matrix products, local(): jnp.einsum('eij,ej->ei', schur_blocks, element_in, precision=lax.Precisio...  6.32 us
    ppermute x2, starting transfers between devices, passed_along(): lax.ppermute(value, axis, [(source, source + steps) for source in range(i...  4.9 us
  transfers between devices with their start and end apart: 6, of which 2 were waited for; matrix products, arithmetic and copies ran while one was open for 9% of the time, Pallas kernels for 0%

commit v1 on v0

--- a/solution.py
+++ b/solution.py
@@ -29,6 +29,19 @@
     count = lax.axis_size(axis)
     initial, last = (max(0, -steps), min(count, count - steps))
     return lax.ppermute(value, axis, [(source, source + steps) for source in range(initial, last)])
+
+
+def summed(value, axes):
+    for axis in axes:
+        count, distance = (lax.axis_size(axis), 1)
+        if count & (count - 1):
+            value = lax.psum(value, axis)
+            continue
+        while distance < count:
+            swap = [(i, i ^ distance) for i in range(count)]
+            value = value + lax.ppermute(value, axis, swap)
+            distance *= 2
+    return value
 
 
 def local(
@@ -79,19 +92,22 @@
     owner_mask = (
         jnp.ones((piece_len,), jnp.float32).at[left_slots[0]].set(jnp.where(left_active, 0.0, 1.0))
     )
-    weighted = owner_mask * residual
-    old_norm, curvature = lax.psum(
-        (
-            jnp.sum(weighted * inverse_diagonal * residual),
+    scaled = owner_mask * inverse_diagonal
+    partial = jnp.stack(
+        [
+            jnp.sum(scaled * residual * residual),
             jnp.sum(owner_mask * direction * applied),
-        ),
-        ("dom", "batch", "sub"),
+            jnp.sum(scaled * residual * applied),
+            jnp.sum(scaled * applied * applied),
+        ]
     )
+    total = summed(partial, ("sub", "batch", "dom"))
+    old_norm, curvature, cross, square = (total[i] for i in range(4))
     step_size = old_norm / curvature
     new_solution = solution + step_size * direction
     new_residual = residual - step_size * applied
     precond = inverse_diagonal * new_residual
-    new_norm = lax.psum(jnp.sum(owner_mask * new_residual * precond), ("dom", "batch", "sub"))
+    new_norm = old_norm - step_size * (2.0 * cross - step_size * square)
     new_direction = precond + new_norm / old_norm * direction
     return (new_solution, new_residual, new_direction)
 

time: 126 us -> 84.5 us (0.67)
  blocking collectives: 63.6 us -> 0 us
  other arithmetic: 26.2 us -> 33.3 us
  waiting for transfers between devices: 2.19 us -> 8.99 us
  starting transfers between devices: 8.12 us -> 13.9 us
  between operations: 3.5 us -> 4.93 us
    psum x2 -> x0, blocking collectives: 63.6 us -> none  [the longest x1 33.5 us: local(): lax.psum((jnp.sum(weighted * inverse_diagonal * residual), jnp.sum(owner_...]
    ppermute x0 -> x4, waiting for transfers between devices: none -> 6.86 us  [summed(): value = value + lax.ppermute(value, axis, swap)]
    ppermute x0 -> x4, starting transfers between devices: none -> 5.79 us  [summed(): value = value + lax.ppermute(value, axis, swap)]
    add x0 -> x4, other arithmetic: none -> 5.41 us  [summed(): value = value + lax.ppermute(value, axis, swap)]
    another operation x0 -> x1, other arithmetic: none -> 2.7 us  [local(): jnp.stack([jnp.sum(scaled * residual * residual), jnp.sum(owner_mask * di...]
  transfers between devices with their start and end apart: 6 -> 10, of which waited for: 2 -> 6; matrix products, arithmetic and copies ran while one was open for 9% -> 14% of each run, Pallas kernels for 0% -> 0%
where the time goes in v1:
time: 84.5 us; the launch traced here: 83.9 us
  other arithmetic  33.3 us (39%)
  local copies, waits for them, and re-layouts  16.5 us (20%)
  starting transfers between devices  13.9 us (16%)
  waiting for transfers between devices  8.99 us (11%)
  matrix products  6.32 us (7%)
  between operations  4.93 us (6%)
    scatter-add x1, other arithmetic, local(): window_sum = jnp.zeros((3 * piece_len,), jnp.float32).at[relative.reshape...  12.3 us
    gather x2, local copies, waits for them, and re-layouts, local(): element_in = jnp.take(window, relative, axis=0)  10.2 us
    ppermute x4, waiting for transfers between devices, summed(): value = value + lax.ppermute(value, axis, swap)  6.86 us
    dot_general x1, matrix products, local(): jnp.einsum('eij,ej->ei', schur_blocks, element_in, precision=lax.Precisio...  6.32 us
    ppermute x4, starting transfers between devices, summed(): value = value + lax.ppermute(value, axis, swap)  5.79 us
    add x4, other arithmetic, summed(): value = value + lax.ppermute(value, axis, swap)  5.41 us
    ppermute x2, starting transfers between devices, passed_along(): lax.ppermute(value, axis, [(source, source + steps) for source in range(i...  4.97 us
    another operation x1, other arithmetic, local(): jnp.stack([jnp.sum(scaled * residual * residual), jnp.sum(owner_mask * di...  2.7 us
  transfers between devices with their start and end apart: 10, of which 6 were waited for; matrix products, arithmetic and copies ran while one was open for 14% of the time, Pallas kernels for 0%

profile of v1, /device:TPU:0, one launch (start us, length us, event | category | flops | bytes accessed | tf_op | source)
XLA Modules:
  0.0 83.9 jit_solution(15942863593426080847)
XLA Ops:
  0.6 0.5 collective-permute-start
  1.1 2.0 %collective-permute-start.1 = (f32[1024]{0:T(1024)}, f32[1024]{0:T(1024)S(1)}, u32[]{:S(2)}, u32[]{:S(2)}) collective-permute-start(f32[1024]{0:T(1024)} %param.12), channel_id=1, source_target_pairs={{1,0},{2,1},{3,2},{0,3},{5,4},{6,5},{7,6},{4,7},{9,8},{10,9},{11,1... | collective-permute-start | bytes 12296 | tf_op jit(solution)/shard_map/ppermute | solution.py:17
  3.1 0.7 compare_select_fusion.1
  3.8 0.1 reshape.108
  3.9 0.7 and_select_fusion
  4.6 0.1 reshape.104
  4.7 0.7 compare_select_fusion.2
  5.4 1.3 %fusion.19 = (s32[1,1]{1,0:T(1,128)}, s32[1,1]{1,0:T(1,128)}) fusion(s32[1,2]{1,0:T(1,128)} %param.19), kind=kLoop, calls=%fused_computation.53 | loop fusion | bytes 16 | tf_op jit(solution)/shard_map/slice | solution.py:85
  6.7 0.7 compare_select_fusion.3
  7.4 0.0 collective-permute-done.1
  7.4 0.7 pad_maximum_fusion
  8.1 10.1 %gather_fusion = f32[1806]{0:T(1024)S(1)} fusion(f32[3072]{0:T(1024)S(1)} %pad_maximum_fusion, s32[2048]{0:T(1024)S(1)} %pad_clamp_fusion), kind=kCustom, calls=%fused_computation | custom fusion | bytes 21672 | tf_op jit(solution)/shard_map/jit(_take)/gather | solution.py:69
  18.2 0.1 reshape.107
  18.3 0.1 select_bitcast_fusion
  18.4 6.3 %fusion.2 = f32[3,1,602]{2,1,0:T(1,128)S(1)} fusion(f32[3,602,602]{2,1,0:T(8,128)} %param.14, f32[3,602,1]{1,0,2:T(4,128)S(1)} %select_bitcast_fusion), kind=kOutput, calls=%fused_computation.19 | convolution fusion | flops 13046544 | bytes 4363296 | tf_op jit(solution)/shard_map/eij,ej->ei/dot_general | solution.py:71
  24.7 0.1 bitcast_select_fusion
  24.8 0.1 reshape.142
  24.9 12.3 %scatter_custom_fusion.1 = f32[3072]{0:T(1024)S(1)} fusion(s32[1806]{0:T(1024)S(1)} %fusion.1, f32[1806]{0:T(1024)S(1)} %reshape.142, f32[]{:T(128)} %constant.68.clone.1), kind=kCustom, calls=%fused_computation.22 | custom fusion | flops 1806 | bytes 12292 | tf_op jit(solution)/shard_map/scatter-add | solution.py:78
  37.2 0.5 collective-permute-start.2
  37.7 0.1 collective-permute-start.3
  37.9 0.6 fusion.14
  38.5 1.4 %scatter_custom_fusion = f32[1024]{0:T(1024)S(1)} fusion(s32[256]{0:T(256)S(1)} %bitcast.24, f32[256]{0:T(256)S(1)} %fusion.14, f32[]{:T(128)} %constant.38.clone.1), kind=kCustom, calls=%fused_computation.37 | custom fusion | bytes 4100 | tf_op jit(solution)/shard_map/scatter | solution.py:93
  39.9 1.0 %collective-permute-done.3 = f32[1024]{0:T(1024)S(1)} collective-permute-done((f32[1024]{0:T(1024)S(1)}, f32[1024]{0:T(1024)S(1)}, u32[]{:S(2)}, u32[]{:S(2)}) %collective-permute-start.3) | collective-permute-done | bytes 4128 | tf_op jit(solution)/shard_map/ppermute | solution.py:25
  40.9 1.4 %gather_fusion.1 = f32[256]{0:T(256)S(1)} fusion(f32[1024]{0:T(1024)S(1)} %fusion.7, s32[1024]{0:T(1024)S(1)} %pad_clamp_fusion.2), kind=kCustom, calls=%fused_computation.1 | custom fusion | bytes 3072 | tf_op jit(solution)/shard_map/gather | solution.py:86
  42.3 0.7 fusion.11
  42.9 3.7 %collective-permute-start.4 = (f32[256]{0:T(256)S(1)}, f32[256]{0:T(256)S(1)}, u32[]{:S(2)}, u32[]{:S(2)}) collective-permute-start(f32[256]{0:T(256)S(1)} %fusion.11), channel_id=1, source_target_pairs={{0,4},{4,8},{8,12},{1,5},{5,9},{9,13},{2,6},{6,10},{10,14},{3,7},{... | collective-permute-start | bytes 3080 | tf_op jit(solution)/shard_map/ppermute | solution.py:31
  46.6 1.4 %gather_fusion.2 = f32[256]{0:T(256)S(1)} fusion(f32[1024]{0:T(1024)S(1)} %fusion.7, s32[1024]{0:T(1024)S(1)} %pad_clamp_fusion.1), kind=kCustom, calls=%fused_computation.2 | custom fusion | bytes 3072 | tf_op jit(solution)/shard_map/gather | solution.py:87
  48.0 0.7 fusion.12
  48.6 1.3 %collective-permute-start.5 = (f32[256]{0:T(256)S(1)}, f32[256]{0:T(256)S(1)}, u32[]{:S(2)}, u32[]{:S(2)}) collective-permute-start(f32[256]{0:T(256)S(1)} %fusion.12), channel_id=1, source_target_pairs={{4,0},{8,4},{12,8},{5,1},{9,5},{13,9},{6,2},{10,6},{14,10},{7,3},{... | collective-permute-start | bytes 3080 | tf_op jit(solution)/shard_map/ppermute | solution.py:31
  50.0 0.7 fusion.13
  50.6 2.3 %scatter_fusion = f32[1024]{0:T(1024)S(1)} fusion(f32[1024]{0:T(1024)S(1)} %fusion.7, s32[256]{0:T(256)S(1)} %bitcast.25, f32[256]{0:T(256)S(1)} %fusion.13), kind=kCustom, calls=%fused_computation.5 | custom fusion | flops 256 | bytes 4096 | tf_op jit(solution)/shard_map/scatter-add | solution.py:90
  52.9 1.2 %collective-permute-done.5 = f32[256]{0:T(256)S(1)} collective-permute-done((f32[256]{0:T(256)S(1)}, f32[256]{0:T(256)S(1)}, u32[]{:S(2)}, u32[]{:S(2)}) %collective-permute-start.5) | collective-permute-done | bytes 1056 | tf_op jit(solution)/shard_map/ppermute | solution.py:31
  54.1 0.6 fusion.10
  54.8 2.3 %scatter_fusion.1 = f32[1024]{0:T(1024)S(1)} fusion(f32[1024]{0:T(1024)S(1)} %scatter_fusion, s32[256]{0:T(256)S(1)} %bitcast.22, f32[256]{0:T(256)S(1)} %fusion.10), kind=kCustom, calls=%fused_computation.6 | custom fusion | flops 256 | bytes 4096 | tf_op jit(solution)/shard_map/scatter-add | solution.py:91
  57.1 0.7 multiply_reduce_fusion.2
  57.8 2.7 %pad_maximum_fusion.1 = f32[4]{0:T(128)S(1)} fusion(f32[1]{0:T(128)} %bitcast.11, f32[1]{0:T(128)} %bitcast.10, f32[1]{0:T(128)} %bitcast.9, f32[1]{0:T(128)} %bitcast.3), kind=kLoop, calls=%fused_computation.50 | loop fusion | flops 12 | bytes 32 | tf_op jit(solution)/shard_map/stack | solution.py:96
  60.5 0.0 collective-permute-start.6
  60.5 1.1 %collective-permute-done.6 = f32[4]{0:T(128)S(1)} collective-permute-done((f32[4]{0:T(128)S(1)}, f32[4]{0:T(128)S(1)}, u32[]{:S(2)}, u32[]{:S(2)}) %collective-permute-start.6) | collective-permute-done | bytes 48 | tf_op jit(solution)/shard_map/ppermute | solution.py:42
  61.6 2.7 %fusion.21 = f32[4]{0:T(128)S(1)} fusion(f32[4]{0:T(128)S(1)} %collective-permute-done.6, f32[1]{0:T(128)} %bitcast.11, f32[1]{0:T(128)} %bitcast.10, f32[1]{0:T(128)} %bitcast.9, f32[1]{0:T(128)} %bitcast.3), kind=kLoop, calls=%fused_computation.54 | loop fusion | flops 16 | bytes 48 | tf_op jit(solution)/shard_map/add | solution.py:42
  64.3 1.5 %collective-permute-start.7 = (f32[4]{0:T(128)S(1)}, f32[4]{0:T(128)S(1)}, u32[]{:S(2)}, u32[]{:S(2)}) collective-permute-start(f32[4]{0:T(128)S(1)} %fusion.21), channel_id=1, source_target_pairs={{0,2},{2,0},{1,3},{3,1},{4,6},{6,4},{5,7},{7,5},{8,10},{10,8},{9,1... | collective-permute-start | bytes 56 | tf_op jit(solution)/shard_map/ppermute | solution.py:42
  65.9 2.0 %collective-permute-done.7 = f32[4]{0:T(128)S(1)} collective-permute-done((f32[4]{0:T(128)S(1)}, f32[4]{0:T(128)S(1)}, u32[]{:S(2)}, u32[]{:S(2)}) %collective-permute-start.7) | collective-permute-done | bytes 48 | tf_op jit(solution)/shard_map/ppermute | solution.py:42
  67.9 2.7 %fusion.22 = f32[4]{0:T(128)S(1)} fusion(f32[4]{0:T(128)S(1)} %collective-permute-done.7, f32[4]{0:T(128)S(1)} %collective-permute-done.6, f32[1]{0:T(128)} %bitcast.11, f32[1]{0:T(128)} %bitcast.10, f32[1]{0:T(128)} %bitcast.9, f32[1]{0:T(128)} %bitcast.3), kind=kLoop, calls=%fused_computation.55 | loop fusion | flops 20 | bytes 64 | tf_op jit(solution)/shard_map/add | solution.py:42
  70.6 1.6 %collective-permute-start.8 = (f32[4]{0:T(128)S(1)}, f32[4]{0:T(128)S(1)}, u32[]{:S(2)}, u32[]{:S(2)}) collective-permute-start(f32[4]{0:T(128)S(1)} %fusion.22), channel_id=1, source_target_pairs={{0,4},{4,0},{8,12},{12,8},{1,5},{5,1},{9,13},{13,9},{2,6},{6,2},{1... | collective-permute-start | bytes 56 | tf_op jit(solution)/shard_map/ppermute | solution.py:42
  72.2 1.9 %collective-permute-done.8 = f32[4]{0:T(128)S(1)} collective-permute-done((f32[4]{0:T(128)S(1)}, f32[4]{0:T(128)S(1)}, u32[]{:S(2)}, u32[]{:S(2)}) %collective-permute-start.8) | collective-permute-done | bytes 48 | tf_op jit(solution)/shard_map/ppermute | solution.py:42
  74.1 2.6 %collective-permute-start.9 = (f32[4]{0:T(128)S(1)}, f32[4]{0:T(128)S(1)}, u32[]{:S(2)}, u32[]{:S(2)}) collective-permute-start(f32[4]{0:T(128)S(1)} %add.117), channel_id=1, source_target_pairs={{0,8},{4,12},{8,0},{12,4},{1,9},{5,13},{9,1},{13,5},{2,10},{6,14},... | collective-permute-start | bytes 56 | tf_op jit(solution)/shard_map/ppermute | solution.py:42
  76.8 1.8 %collective-permute-done.9 = f32[4]{0:T(128)S(1)} collective-permute-done((f32[4]{0:T(128)S(1)}, f32[4]{0:T(128)S(1)}, u32[]{:S(2)}, u32[]{:S(2)}) %collective-permute-start.9) | collective-permute-done | bytes 48 | tf_op jit(solution)/shard_map/ppermute | solution.py:42
  78.6 0.6 fusion.18
  83.3 0.6 multiply_add_fusion
  (19 shorter events, 0.1 us)
Async XLA Ops:
  0.6 6.8 %collective-permute-start = (f32[1024]{0:T(1024)}, f32[1024]{0:T(1024)S(1)}, u32[]{:S(2)}, u32[]{:S(2)}) collective-permute-start(f32[1024]{0:T(1024)} %param.12), channel_id=1, source_target_pairs={{0,1},{1,2},{2,3},{3,0},{4,5},{5,6},{6,7},{7,4},{8,9},{9,10},{10,1... | collective-permute-start | bytes 12296 | tf_op jit(solution)/shard_map/ppermute | solution.py:16
  1.1 6.3 %collective-permute-start.1 = (f32[1024]{0:T(1024)}, f32[1024]{0:T(1024)S(1)}, u32[]{:S(2)}, u32[]{:S(2)}) collective-permute-start(f32[1024]{0:T(1024)} %param.12), channel_id=1, source_target_pairs={{1,0},{2,1},{3,2},{0,3},{5,4},{6,5},{7,6},{4,7},{9,8},{10,9},{11,1... | collective-permute-start | bytes 12296 | tf_op jit(solution)/shard_map/ppermute | solution.py:17
  18.4 38.7 %copy-start = (f32[1024]{0:T(1024)S(1)}, f32[1024]{0:T(1024)}, u32[]{:S(2)}) copy-start(f32[1024]{0:T(1024)} %param.12) | copy-start | bytes 12292
  18.4 38.7 %copy-start.1 = (f32[1024]{0:T(1024)S(1)}, f32[1024]{0:T(1024)}, u32[]{:S(2)}) copy-start(f32[1024]{0:T(1024)} %param.13) | copy-start | bytes 12292
  18.4 38.7 %copy-start.2 = (f32[1024]{0:T(1024)S(1)}, f32[1024]{0:T(1024)}, u32[]{:S(2)}) copy-start(f32[1024]{0:T(1024)} %param.11) | copy-start | bytes 12292
  18.4 64.9 %copy-start.3 = (f32[1024]{0:T(1024)S(1)}, f32[1024]{0:T(1024)}, u32[]{:S(2)}) copy-start(f32[1024]{0:T(1024)} %param.10) | copy-start | bytes 12292
  37.2 2.7 %collective-permute-start.2 = (f32[1024]{0:T(1024)S(1)}, f32[1024]{0:T(1024)S(1)}, u32[]{:S(2)}, u32[]{:S(2)}) collective-permute-start(f32[1024]{0:T(1024)S(1)} %get-tuple-element.11), channel_id=1, source_target_pairs={{1,0},{2,1},{3,2},{0,3},{5,4},{6,5},{7,6},{4,7},{9,8},{10,9},{11,1... | collective-permute-start | bytes 12296 | tf_op jit(solution)/shard_map/ppermute | solution.py:25
  37.7 3.1 %collective-permute-start.3 = (f32[1024]{0:T(1024)S(1)}, f32[1024]{0:T(1024)S(1)}, u32[]{:S(2)}, u32[]{:S(2)}) collective-permute-start(f32[1024]{0:T(1024)S(1)} %get-tuple-element.12), channel_id=1, source_target_pairs={{3,0},{0,1},{1,2},{2,3},{7,4},{4,5},{5,6},{6,7},{11,8},{8,9},{9,10... | collective-permute-start | bytes 12296 | tf_op jit(solution)/shard_map/ppermute | solution.py:25
  42.9 7.0 %collective-permute-start.4 = (f32[256]{0:T(256)S(1)}, f32[256]{0:T(256)S(1)}, u32[]{:S(2)}, u32[]{:S(2)}) collective-permute-start(f32[256]{0:T(256)S(1)} %fusion.11), channel_id=1, source_target_pairs={{0,4},{4,8},{8,12},{1,5},{5,9},{9,13},{2,6},{6,10},{10,14},{3,7},{... | collective-permute-start | bytes 3080 | tf_op jit(solution)/shard_map/ppermute | solution.py:31
  48.6 5.5 %collective-permute-start.5 = (f32[256]{0:T(256)S(1)}, f32[256]{0:T(256)S(1)}, u32[]{:S(2)}, u32[]{:S(2)}) collective-permute-start(f32[256]{0:T(256)S(1)} %fusion.12), channel_id=1, source_target_pairs={{4,0},{8,4},{12,8},{5,1},{9,5},{13,9},{6,2},{10,6},{14,10},{7,3},{... | collective-permute-start | bytes 3080 | tf_op jit(solution)/shard_map/ppermute | solution.py:31
  60.5 1.1 %collective-permute-start.6 = (f32[4]{0:T(128)S(1)}, f32[4]{0:T(128)S(1)}, u32[]{:S(2)}, u32[]{:S(2)}) collective-permute-start(f32[4]{0:T(128)S(1)} %pad_maximum_fusion.1), channel_id=1, source_target_pairs={{0,1},{1,0},{2,3},{3,2},{4,5},{5,4},{6,7},{7,6},{8,9},{9,8},{10,11... | collective-permute-start | bytes 56 | tf_op jit(solution)/shard_map/ppermute | solution.py:42
  64.3 3.5 %collective-permute-start.7 = (f32[4]{0:T(128)S(1)}, f32[4]{0:T(128)S(1)}, u32[]{:S(2)}, u32[]{:S(2)}) collective-permute-start(f32[4]{0:T(128)S(1)} %fusion.21), channel_id=1, source_target_pairs={{0,2},{2,0},{1,3},{3,1},{4,6},{6,4},{5,7},{7,5},{8,10},{10,8},{9,1... | collective-permute-start | bytes 56 | tf_op jit(solution)/shard_map/ppermute | solution.py:42
  70.6 3.5 %collective-permute-start.8 = (f32[4]{0:T(128)S(1)}, f32[4]{0:T(128)S(1)}, u32[]{:S(2)}, u32[]{:S(2)}) collective-permute-start(f32[4]{0:T(128)S(1)} %fusion.22), channel_id=1, source_target_pairs={{0,4},{4,0},{8,12},{12,8},{1,5},{5,1},{9,13},{13,9},{2,6},{6,2},{1... | collective-permute-start | bytes 56 | tf_op jit(solution)/shard_map/ppermute | solution.py:42
  74.1 4.4 %collective-permute-start.9 = (f32[4]{0:T(128)S(1)}, f32[4]{0:T(128)S(1)}, u32[]{:S(2)}, u32[]{:S(2)}) collective-permute-start(f32[4]{0:T(128)S(1)} %add.117), channel_id=1, source_target_pairs={{0,8},{4,12},{8,0},{12,4},{1,9},{5,13},{9,1},{13,5},{2,10},{6,14},... | collective-permute-start | bytes 56 | tf_op jit(solution)/shard_map/ppermute | solution.py:42

commit v2 on v0

v2 whole, which is shorter than its diff:
```python
import functools

import jax
import jax.numpy as jnp
from jax import lax
from jax.experimental import pallas as pl
from jax.experimental.pallas import tpu as pltpu
from jax.sharding import PartitionSpec as P

ORDER = 10
LANES = 128
VMEM_LIMIT = 32 * 1024 * 1024
SUMS = 24
STATIC = 48


def split(value):
    high = value.astype(jnp.bfloat16).astype(jnp.float32)
    rest = value - high
    middle = rest.astype(jnp.bfloat16).astype(jnp.float32)
    return [high, middle, rest - middle]


def half(value):
    return value.astype(jnp.bfloat16)


def pick(table, lane_hot, row_hot):
    rows = table.shape[0]
    parts = jnp.dot(
        half(jnp.concatenate(split(table), axis=0)), lane_hot, preferred_element_type=jnp.float32
    )
    found = (parts[:rows] + parts[rows : 2 * rows]) + parts[2 * rows :]
    return jnp.sum(found * row_hot, axis=0, keepdims=True)


def place(values, lane_hot, row_hot):
    rows = row_hot.shape[0]
    spread = jnp.concatenate([row_hot * part for part in split(values)], axis=0)
    parts = lax.dot_general(
        half(spread), lane_hot, (((1,), (1,)), ((), ())), preferred_element_type=jnp.float32
    )
    return (parts[:rows] + parts[rows : 2 * rows]) + parts[2 * rows :]


def hot(index, count):
    rows = lax.broadcasted_iota(jnp.int32, (count, index.shape[1]), 0)
    return jnp.where(rows == index, 1.0, 0.0)


def as_rows(row):
    return [row[:, i * LANES : (i + 1) * LANES] for i in range(row.shape[1] // LANES)]


def as_row(rows):
    return jnp.concatenate([rows[i : i + 1] for i in range(rows.shape[0])], axis=1)


def prepare_kernel(
    group_axes,
    order_ref,
    count_ref,
    dofs_ref,
    left_ref,
    right_ref,
    direction_ref,
    residual_ref,
    diagonal_ref,
    blocks_hbm,
    blocks_ref,
    lane_ref,
    row_ref,
    pair_lane_ref,
    pair_row_ref,
    static_ref,
    index_ref,
    sem,
):
    copy = pltpu.make_async_copy(blocks_hbm, blocks_ref, sem)
    copy.start()
    (outer, inner) = group_axes
    me = lax.axis_index(outer) * lax.axis_size(inner) + lax.axis_index(inner)
    elements, size = dofs_ref.shape
    width = index_ref.shape[1]
    rows = direction_ref.shape[0]
    slot_bits = (rows * LANES - 1).bit_length()
    lane_bits = LANES.bit_length() - 1
    index_ref[...] = jnp.full(index_ref.shape, -1, jnp.int32)
    index_ref[:elements, :size] = dofs_ref[...]
    lanes = lax.broadcasted_iota(jnp.int32, (1, width), 1)
    for e in range(elements):
        order = order_ref[e]
        live = size * (6 * order * order + 2) // (6 * ORDER * ORDER + 2)
        active = lanes < live
        dofs = index_ref[e : e + 1, :]
        piece = lax.shift_right_logical(dofs, slot_bits)
        place_of = jnp.where(piece == me, 0, jnp.where(piece == (me ^ 1), 1, 2))
        high = place_of * rows + (lax.shift_right_logical(dofs, lane_bits) & (rows - 1))
        low = jnp.where(active, dofs & (LANES - 1), -1)
        high = jnp.where(active, high, -1)
        lane_ref[:, e * width : (e + 1) * width] = half(hot(low, LANES))
        row_ref[:, e * width : (e + 1) * width] = hot(high, 3 * rows)
    pairs = left_ref.shape[1]
    pair_lanes = lax.broadcasted_iota(jnp.int32, (1, pairs), 1)
    right = jnp.where(pair_lanes < count_ref[0, 1], right_ref[...], -1)
    left = jnp.where(pair_lanes < count_ref[0, 0], left_ref[...], -1)
    slots = jnp.concatenate([right, left], axis=1)
    pair_lane = half(hot(jnp.where(slots < 0, -1, slots & (LANES - 1)), LANES))
    pair_row = hot(lax.shift_right_arithmetic(slots, lane_bits), rows)
    pair_lane_ref[...] = pair_lane
    pair_row_ref[...] = pair_row
    shared = lax.dot_general(
        half(pair_row[:, pairs:]),
        pair_lane[:, pairs:],
        (((1,), (1,)), ((), ())),
        preferred_element_type=jnp.float32,
    )
    owner = 1.0 - shared
    direction = direction_ref[...]
    diagonal = diagonal_ref[...]
    scaled = diagonal * residual_ref[...]
    static_ref[0:8] = owner * diagonal
    static_ref[8:16] = owner * direction
    static_ref[16:24] = owner * scaled
    static_ref[24:32] = owner * scaled * residual_ref[...]
    lines = []
    for table in (direction, scaled, diagonal):
        lines += as_rows(pick(table, pair_lane[:, :pairs], pair_row[:, :pairs]))
    lines += as_rows(slots.astype(jnp.float32))
    lines += [jnp.zeros((1, LANES), jnp.float32)] * (STATIC - 32 - len(lines))
    static_ref[32:STATIC] = jnp.concatenate(lines, axis=0)
    copy.wait()


def element_kernel(
    own_ref, first_ref, second_ref, blocks_ref, lane_ref, row_ref, static_ref, out_ref, in_ref, y_ref
):
    elements, size, _ = blocks_ref.shape
    width = y_ref.shape[1]
    window = jnp.concatenate([own_ref[...], first_ref[...], second_ref[...]], axis=0)
    element_in = pick(window, lane_ref[...], row_ref[...])
    in_ref[...] = jnp.zeros(in_ref.shape, jnp.float32)
    for e in range(elements):
        in_ref[e : e + 1, :] = element_in[:, e * width : (e + 1) * width]
    columns = in_ref[...].T
    y_ref[...] = jnp.zeros(y_ref.shape, jnp.float32)
    whole = size // 8 * 8
    for e in range(elements):
        total = jnp.zeros((8, size), jnp.float32)
        for start in range(0, whole, 8):
            total += blocks_ref[e, start : start + 8, :] * columns[start : start + 8, e : e + 1]
        total = jnp.sum(total, axis=0, keepdims=True)
        for line in range(whole, size):
            total += blocks_ref[e, line : line + 1, :] * columns[line : line + 1, e : e + 1]
        y_ref[e : e + 1, :size] = total
    element_out = jnp.concatenate([y_ref[e : e + 1, :] for e in range(elements)], axis=1)
    out_ref[:SUMS] = place(element_out, lane_ref[...], row_ref[...])
    out_ref[SUMS:] = static_ref[...]


def sum_kernel(count, *refs):
    messages, (pair_lane_ref, pair_row_ref, own_ref, out_ref) = refs[:count], refs[count:]
    rows = own_ref.shape[0]
    half_pairs = pair_lane_ref.shape[1] // 2
    lines = half_pairs // LANES
    lane_bits = LANES.bit_length() - 1
    totals = [jnp.zeros((rows, LANES), jnp.float32) for _ in range(4)]
    found = [[] for _ in range(5)]
    for m, message in enumerate(messages):
        applied = message[0:8] + messages[m ^ 1][8:16] + messages[m ^ 3][16:24]
        at = functools.partial(lambda ref, i: ref[SUMS + 8 * i : SUMS + 8 * i + 8], message)
        totals[0] += at(3)
        totals[1] += at(1) * applied
        totals[2] += at(2) * applied
        totals[3] += at(0) * applied * applied
        base = SUMS + 32
        if m == 0:
            own_ref[...] = applied
            pair_lane, pair_row = pair_lane_ref[...], pair_row_ref[...]
        else:
            slots = as_row(message[base + 3 * lines : base + 5 * lines]).astype(jnp.int32)
            pair_lane = half(hot(jnp.where(slots < 0, -1, slots & (LANES - 1)), LANES))
            pair_row = hot(lax.shift_right_arithmetic(slots, lane_bits), rows)
        values = as_rows(pick(applied, pair_lane, pair_row))
        found[0] += values[:lines]
        found[1] += values[lines:]
        for i in range(3):
            found[2 + i].append(message[base + i * lines : base + (i + 1) * lines])
    for i in range(4):
        out_ref[i * rows : (i + 1) * rows] = totals[i]
    base, step = 4 * rows, count * lines
    for i in range(5):
        out_ref[base + i * step : base + (i + 1) * step] = jnp.concatenate(found[i], axis=0)


def final_kernel(
    dom_axis,
    inner_axis,
    ordered,
    count,
    lines,
    *refs,
):
    messages = [ref[...] for ref in refs[:count]]
    (
        own_ref,
        pair_lane_ref,
        pair_row_ref,
        solution_ref,
        residual_ref,
        direction_ref,
        diagonal_ref,
        new_solution_ref,
        new_residual_ref,
        new_direction_ref,
    ) = refs[count:]
    rows = own_ref.shape[0]
    me = lax.axis_index(dom_axis)
    if not ordered:
        own, direct, far, relayed = messages
        relayed = other_order(relayed, 4 * rows, lines)
        even = lax.axis_index(inner_axis) == 0
        line = [own, jnp.where(even, direct, relayed), jnp.where(even, relayed, direct), far]
        low = (me & 1) == 0
        high = (me & 2) == 0
        line = [jnp.where(low, line[i], line[i ^ 1]) for i in range(4)]
        messages = [jnp.where(high, line[i], line[i ^ 2]) for i in range(4)]
    base = 4 * rows
    step = (messages[0].shape[0] - base) // 5
    totals = messages[0][:base]
    for message in messages[1:]:
        totals = totals + message[:base]
    old, curve, cross, square = (totals[i * rows : (i + 1) * rows] for i in range(4))

    def part(message, i):
        return message[base + i * step : base + (i + 1) * step]

    from_left = jnp.zeros((lines, LANES), jnp.float32)
    from_right = jnp.zeros((lines, LANES), jnp.float32)
    for d in range(count - 1):
        near, next_one = messages[d], messages[d + 1]
        forward, backward = part(near, 0), part(next_one, 1)
        terms = [
            part(near, 2) * backward,
            part(near, 3) * backward,
            part(near, 4) * backward * (2.0 * forward + backward),
        ]
        for start in range(0, step, rows):
            curve = curve + terms[0][start : start + rows]
            cross = cross + terms[1][start : start + rows]
            square = square + terms[2][start : start + rows]
        from_left = jnp.where(me == d + 1, forward[:lines], from_left)
        from_right = jnp.where(me == d, backward[:lines], from_right)
    incoming = as_row(jnp.concatenate([from_right, from_left], axis=0))
    applied = own_ref[...] + place(incoming, pair_lane_ref[...], pair_row_ref[...])

    def whole(value):
        return jnp.sum(value, axis=(0, 1), keepdims=True)

    old_norm = whole(old)
    step_size = old_norm / whole(curve)
    new_norm = whole(old - step_size * (2.0 * cross - step_size * square))
    direction = direction_ref[...]
    new_residual = residual_ref[...] - step_size * applied
    new_solution_ref[...] = solution_ref[...] + step_size * direction
    new_residual_ref[...] = new_residual
    new_direction_ref[...] = diagonal_ref[...] * new_residual + (new_norm / old_norm) * direction


def other_order(message, base, lines):
    blocks = [message[:base]]
    for start in range(base, message.shape[0], 2 * lines):
        blocks += [message[start + lines : start + 2 * lines], message[start : start + lines]]
    return jnp.concatenate(blocks, axis=0)


def specs(spaces):
    return [pl.BlockSpec(memory_space=space) for space in spaces]


def swap_first(count):
    return [(i, i ^ 1) for i in range(count)]


def swap_second(count):
    return [(i, (i + 1 if i % 2 else i - 1) % count) for i in range(count)]


def local(
    solution,
    residual,
    direction,
    inverse_diagonal,
    schur_blocks,
    elem_dofs,
    element_order,
    left_slots,
    right_slots,
    share_count,
):
    group, dom = ("batch", "sub"), "dom"
    group_count, dom_count = lax.axis_size(group), lax.axis_size(dom)
    sub_count = lax.axis_size("sub")
    elements, size = elem_dofs.shape
    width = -(-size // LANES) * LANES
    pairs = left_slots.shape[1]
    lines = pairs // LANES
    rows = residual.shape[0] // LANES
    f32, bf16 = jnp.float32, jnp.bfloat16
    vmem, smem = pltpu.VMEM, pltpu.SMEM
    params = pltpu.CompilerParams(vmem_limit_bytes=VMEM_LIMIT)

    solution, residual, direction, inverse_diagonal = (
        value.reshape(rows, LANES) for value in (solution, residual, direction, inverse_diagonal)
    )
    first = lax.ppermute(direction, group, swap_first(group_count))
    second = lax.ppermute(direction, group, swap_second(group_count))

    blocks, lane_hot, row_hot, pair_lane, pair_row, static = pl.pallas_call(
        functools.partial(prepare_kernel, group),
        out_shape=[
            jax.ShapeDtypeStruct(schur_blocks.shape, f32),
            jax.ShapeDtypeStruct((LANES, elements * width), bf16),
            jax.ShapeDtypeStruct((3 * rows, elements * width), f32),
            jax.ShapeDtypeStruct((LANES, 2 * pairs), bf16),
            jax.ShapeDtypeStruct((rows, 2 * pairs), f32),
            jax.ShapeDtypeStruct((STATIC, LANES), f32),
        ],
        in_specs=specs([smem, smem] + [vmem] * 6 + [pl.ANY]),
        out_specs=specs([vmem] * 6),
        scratch_shapes=[pltpu.VMEM((8, width), jnp.int32), pltpu.SemaphoreType.DMA],
        compiler_params=params,
        name="prepare",
    )(
        element_order,
        share_count,
        elem_dofs,
        left_slots,
        right_slots,
        direction,
        residual,
        inverse_diagonal,
        schur_blocks,
    )

    message = pl.pallas_call(
        element_kernel,
        out_shape=jax.ShapeDtypeStruct((SUMS + STATIC, LANES), f32),
        in_specs=specs([vmem] * 7),
        out_specs=pl.BlockSpec(memory_space=vmem),
        scratch_shapes=[pltpu.VMEM((8, width), f32), pltpu.VMEM((8, width), f32)],
        compiler_params=params,
        name="elements",
    )(direction, first, second, blocks, lane_hot, row_hot, static)

    if group_count == 4:
        messages = [message] + [
            lax.ppermute(message, group, [(i, i ^ m) for i in range(4)]) for m in (1, 2, 3)
        ]
    else:
        me = lax.axis_index(group)
        order = me ^ jnp.arange(group_count)
        everyone = lax.all_gather(message, group)
        second_of = jnp.array([target for _, target in swap_second(group_count)])
        moved = everyone[second_of[me ^ 3 ^ jnp.arange(group_count)], 2 * rows : 3 * rows]
        everyone = everyone[order].at[:, 2 * rows : 3 * rows].set(moved)
        messages = [everyone[m] for m in range(group_count)]

    own, message = pl.pallas_call(
        functools.partial(sum_kernel, group_count),
        out_shape=[
            jax.ShapeDtypeStruct((rows, LANES), f32),
            jax.ShapeDtypeStruct((4 * rows + 5 * group_count * lines, LANES), f32),
        ],
        in_specs=specs([vmem] * (group_count + 2)),
        out_specs=specs([vmem] * 2),
        compiler_params=params,
        name="sums",
    )(*messages, pair_lane, pair_row)

    ordered = not (dom_count == 4 and sub_count == 2)
    if ordered:
        everyone = lax.all_gather(message, dom)
        messages = [everyone[d] for d in range(dom_count)]
    else:
        line = (dom, "sub")
        near = [(2 * d + s, 2 * (d ^ (1 + s)) + s) for d in range(4) for s in range(2)]
        opposite = [(2 * d + s, 2 * (d ^ 3) + s) for d in range(4) for s in range(2)]
        direct = lax.ppermute(message, line, near)
        far = lax.ppermute(message, line, opposite)
        relayed = lax.ppermute(direct, "sub", [(0, 1), (1, 0)])
        messages = [message, direct, far, relayed]

    outputs = pl.pallas_call(
        functools.partial(final_kernel, dom, "sub", ordered, dom_count, lines),
        out_shape=[jax.ShapeDtypeStruct((rows, LANES), f32)] * 3,
        in_specs=specs([vmem] * (dom_count + 7)),
        out_specs=specs([vmem] * 3),
        compiler_params=params,
        name="update",
    )(*messages, own, pair_lane, pair_row, solution, residual, direction, inverse_diagonal)
    return tuple(value.reshape(-1) for value in outputs)


def solution(mesh):
    whole = P(("groups", "dom", "batch", "sub"))
    lines = P(("groups", "dom", "batch", "sub"), None)
    return jax.shard_map(
        local,
        mesh=mesh,
        in_specs=(whole,) * 4
        + (P(("groups", "dom", "batch", "sub"), None, None), lines, whole, lines, lines, lines),
        out_specs=(whole,) * 3,
        check_vma=False,
    )
```

time: 126 us -> 27.9 us (0.22)
  blocking collectives: 63.6 us -> 0 us
  other arithmetic: 26.2 us -> 0 us
  local copies, waits for them, and re-layouts: 15.9 us -> 7.76 us
  matrix products: 6.32 us -> 0 us
  waiting for transfers between devices: 2.19 us -> 6.08 us
  Pallas kernels: 0 us -> 3.81 us
  between operations: 3.5 us -> 0.7 us
    psum x2 -> x0, blocking collectives: 63.6 us -> none  [the longest x1 33.5 us: local(): lax.psum((jnp.sum(weighted * inverse_diagonal * residual), jnp.sum(owner_...]
    scatter-add x3 -> x0, other arithmetic: 16.9 us -> none  [the longest x1 12.2 us: local(): window_sum = jnp.zeros((3 * piece_len,), jnp.float32).at[relative.reshape...]
    gather x4 -> x0, local copies, waits for them, and re-layouts: 12.9 us -> none  [the longest x2 10.2 us: local(): element_in = jnp.take(window, relative, axis=0)]
    unnamed x8 -> x24, local copies, waits for them, and re-layouts: 0.01 us -> 7.76 us
    dot_general x1 -> x0, matrix products: 6.32 us -> none  [local(): jnp.einsum('eij,ej->ei', schur_blocks, element_in, precision=lax.Precisio...]
    select_n x12 -> x0, other arithmetic: 6.17 us -> none  [the longest x2 1.33 us: local(): forward = jnp.where(right_active, own_rows[right_slots[0]], 0.0)]
    ppermute x6 -> x8, waiting for transfers between devices: 2.19 us -> 6.08 us  [the longest x1 3.21 us: local(): far = lax.ppermute(message, line, opposite)]
    pallas_call x0 -> x4, Pallas kernels: none -> 3.81 us  [the longest x1 1.46 us: local(): pl.pallas_call(functools.partial(prepare_kernel, group), out_shape=[jax.S...]
  transfers between devices with their start and end apart: 6 -> 8, of which waited for: 2 -> 4; matrix products, arithmetic and copies ran while one was open for 9% -> 0% of each run, Pallas kernels for 0% -> 5%
where the time goes in v2:
time: 27.9 us; the launch traced here: 27.5 us
  starting transfers between devices  9.17 us (33%)
  local copies, waits for them, and re-layouts  7.76 us (28%)
  waiting for transfers between devices  6.08 us (22%)
  Pallas kernels  3.81 us (14%)
  between operations  0.7 us (3%)
    unnamed x24, local copies, waits for them, and re-layouts  7.76 us
    ppermute x1, waiting for transfers between devices, local(): far = lax.ppermute(message, line, opposite)  3.21 us
    ppermute x3, waiting for transfers between devices, local(): lax.ppermute(message, group, [(i, i ^ m) for i in range(4)])  2.71 us
    ppermute x1, starting transfers between devices, local(): far = lax.ppermute(message, line, opposite)  2.48 us
    ppermute x1, starting transfers between devices, local(): second = lax.ppermute(direction, group, swap_second(group_count))  2.44 us
    ppermute x3, starting transfers between devices, local(): lax.ppermute(message, group, [(i, i ^ m) for i in range(4)])  1.93 us
    ppermute x1, starting transfers between devices, local(): direct = lax.ppermute(message, line, near)  1.64 us
    pallas_call x1, Pallas kernels, local(): pl.pallas_call(functools.partial(prepare_kernel, group), out_shape=[jax.S...  1.46 us
  transfers between devices with their start and end apart: 8, of which 4 were waited for; matrix products, arithmetic and copies ran while one was open for 0% of the time, Pallas kernels for 5%

profile of v2, /device:TPU:0, one launch (start us, length us, event | category | flops | bytes accessed | tf_op | source)
XLA Modules:
  0.0 27.5 jit_solution(6240221424743133279)
XLA Ops:
  0.6 2.4 %collective-permute-start.1 = (f32[8,128]{1,0:T(8,128)}, f32[8,128]{1,0:T(8,128)S(1)}, u32[]{:S(2)}, u32[]{:S(2)}) collective-permute-start(f32[8,128]{1,0:T(8,128)} %bitcast.7), channel_id=1, source_target_pairs={{0,3},{1,2},{2,1},{3,0},{4,7},{5,6},{6,5},{7,4},{8,11},{9,10},{10,... | collective-permute-start | bytes 12296 | tf_op jit(solution)/shard_map/ppermute | solution.py:317
  3.1 0.7 %collective-permute-start = (f32[8,128]{1,0:T(8,128)}, f32[8,128]{1,0:T(8,128)S(1)}, u32[]{:S(2)}, u32[]{:S(2)}) collective-permute-start(f32[8,128]{1,0:T(8,128)} %bitcast.8), channel_id=1, source_target_pairs={{0,1},{1,0},{2,3},{3,2},{4,5},{5,4},{6,7},{7,6},{8,9},{9,8},{10,11... | collective-permute-start | bytes 12296 | tf_op jit(solution)/shard_map/ppermute | solution.py:316
  3.8 0.0 copy-start
  3.8 2.3 %copy-done = f32[3,602,602]{2,1,0:T(8,128)S(1)} copy-done((f32[3,602,602]{2,1,0:T(8,128)S(1)}, f32[3,602,602]{2,1,0:T(8,128)}, u32[]{:S(2)}) %copy-start) | copy-done | bytes 4348872
  6.1 0.0 copy-start.1
  6.1 0.7 %copy-done.1 = f32[1024]{0:T(1024)S(1)} copy-done((f32[1024]{0:T(1024)S(1)}, f32[1024]{0:T(1024)}, u32[]{:S(2)}) %copy-start.1) | copy-done | bytes 4120
  6.8 0.0 copy-start.2
  6.8 0.7 %copy-done.2 = f32[1024]{0:T(1024)S(1)} copy-done((f32[1024]{0:T(1024)S(1)}, f32[1024]{0:T(1024)}, u32[]{:S(2)}) %copy-start.2) | copy-done | bytes 4120
  7.5 0.0 copy-start.4
  7.5 0.7 %copy-done.4 = f32[1024]{0:T(1024)S(1)} copy-done((f32[1024]{0:T(1024)S(1)}, f32[1024]{0:T(1024)}, u32[]{:S(2)}) %copy-start.4) | copy-done | bytes 4120
  8.1 0.0 copy-start.6
  8.1 0.7 %copy-done.6 = s32[3,602]{1,0:T(4,128)S(1)} copy-done((s32[3,602]{1,0:T(4,128)S(1)}, s32[3,602]{1,0:T(4,128)}, u32[]{:S(2)}) %copy-start.6) | copy-done | bytes 7248
  8.8 0.0 copy-start.8
  8.8 0.7 %copy-done.8 = s32[1,256]{1,0:T(1,128)S(1)} copy-done((s32[1,256]{1,0:T(1,128)S(1)}, s32[1,256]{1,0:T(1,128)}, u32[]{:S(2)}) %copy-start.8) | copy-done | bytes 1048
  9.5 0.0 copy-start.9
  9.5 0.7 %copy-done.9 = s32[1,256]{1,0:T(1,128)S(1)} copy-done((s32[1,256]{1,0:T(1,128)S(1)}, s32[1,256]{1,0:T(1,128)}, u32[]{:S(2)}) %copy-start.9) | copy-done | bytes 1048
  10.2 0.0 copy-start.10
  10.2 0.7 %copy-done.10 = s32[3]{0:T(128)S(1)} copy-done((s32[3]{0:T(128)S(1)}, s32[3]{0:T(128)}, u32[]{:S(2)}) %copy-start.10) | copy-done | bytes 36
  10.9 0.0 copy-start.11
  10.9 0.7 %copy-done.11 = s32[1,2]{1,0:T(1,128)S(1)} copy-done((s32[1,2]{1,0:T(1,128)S(1)}, s32[1,2]{1,0:T(1,128)}, u32[]{:S(2)}) %copy-start.11) | copy-done | bytes 32
  11.5 0.0 copy-start.3
  11.5 0.0 copy-start.5
  11.5 0.0 copy-start.7
  11.5 1.5 %prepare.1 = (f32[3,602,602]{2,1,0:T(8,128)S(1)}, bf16[128,1920]{1,0:T(8,128)(2,1)S(1)}, f32[24,1920]{1,0:T(8,128)S(1)}, bf16[128,512]{1,0:T(8,128)(2,1)S(1)}, f...) custom-call(s32[3]{0:T(128)S(1)} %copy-done.10, s32[1,2]{1,0:T(1,128)S(1)} %copy-done.11, s32[3,602]{1,0:T(4,128)S(1)} %copy-done.6, ...), custom_call_target="tpu_custom_call" | custom-call | tf_op jit(solution)/shard_map/prepare/pallas_call | solution.py:319
  13.0 0.0 collective-permute-done.1.second_ref
  13.0 0.0 collective-permute-done.first_ref
  13.0 1.3 %elements.1.refs_0_ = f32[72,128]{1,0:T(8,128)S(1)} custom-call(f32[8,128]{1,0:T(8,128)S(1)} %bitcast.10, f32[8,128]{1,0:T(8,128)S(1)} %collective-permute-done.first_ref, f32[8,128]{1,0:T(8,128)S(1)} %collective-permute-done.1.second_ref, f32[3,602,602]{2,1,0:T(8,128)S(1)} %get-tuple-element.14.blocks_ref, ...), custom_call_target="tpu_custom_call" | custom-call | tf_op jit(solution)/shard_map/elements/pallas_call | solution.py:346
  14.3 0.1 collective-permute-start.4
  14.4 1.6 %collective-permute-start.3 = (f32[72,128]{1,0:T(8,128)S(1)}, f32[72,128]{1,0:T(8,128)S(1)}, u32[]{:S(2)}, u32[]{:S(2)}) collective-permute-start(f32[72,128]{1,0:T(8,128)S(1)} %elements.1.refs_0_), channel_id=1, source_target_pairs={{0,2},{1,3},{2,0},{3,1},{4,6},{5,7},{6,4},{7,5},{8,10},{9,11},{10,... | collective-permute-start | bytes 110600 | tf_op jit(solution)/shard_map/ppermute | solution.py:358
  16.0 0.2 collective-permute-start.2
  16.2 1.7 %collective-permute-done.4.refs_3_ = f32[72,128]{1,0:T(8,128)S(1)} collective-permute-done((f32[72,128]{1,0:T(8,128)S(1)}, f32[72,128]{1,0:T(8,128)S(1)}, u32[]{:S(2)}, u32[]{:S(2)}) %collective-permute-start.4) | collective-permute-done | bytes 36896 | tf_op jit(solution)/shard_map/ppermute | solution.py:358
  17.9 1.0 %collective-permute-done.3.refs_2_ = f32[72,128]{1,0:T(8,128)S(1)} collective-permute-done((f32[72,128]{1,0:T(8,128)S(1)}, f32[72,128]{1,0:T(8,128)S(1)}, u32[]{:S(2)}, u32[]{:S(2)}) %collective-permute-start.3) | collective-permute-done | bytes 36896 | tf_op jit(solution)/shard_map/ppermute | solution.py:358
  18.9 0.0 collective-permute-done.2.refs_1_
  18.9 0.2 sums.1
  19.1 1.6 %collective-permute-start.5 = (f32[72,128]{1,0:T(8,128)S(1)}, f32[72,128]{1,0:T(8,128)S(1)}, u32[]{:S(2)}, u32[]{:S(2)}) collective-permute-start(f32[72,128]{1,0:T(8,128)S(1)} %get-tuple-element.20.refs_0_), channel_id=1, source_target_pairs={{0,4},{1,9},{4,0},{5,13},{8,12},{9,1},{12,8},{13,5},{2,6},{3,11},{... | collective-permute-start | bytes 110600 | tf_op jit(solution)/shard_map/ppermute | solution.py:389
  20.8 2.5 %collective-permute-start.6 = (f32[72,128]{1,0:T(8,128)S(1)}, f32[72,128]{1,0:T(8,128)S(1)}, u32[]{:S(2)}, u32[]{:S(2)}) collective-permute-start(f32[72,128]{1,0:T(8,128)S(1)} %get-tuple-element.20.refs_0_), channel_id=1, source_target_pairs={{0,12},{1,13},{4,8},{5,9},{8,4},{9,5},{12,0},{13,1},{2,14},{3,15},... | collective-permute-start | bytes 110600 | tf_op jit(solution)/shard_map/ppermute | solution.py:390
  23.3 0.2 collective-permute-done.5.refs_1_
  23.4 0.0 collective-permute-start.7
  23.4 3.2 %collective-permute-done.6.refs_2_ = f32[72,128]{1,0:T(8,128)S(1)} collective-permute-done((f32[72,128]{1,0:T(8,128)S(1)}, f32[72,128]{1,0:T(8,128)S(1)}, u32[]{:S(2)}, u32[]{:S(2)}) %collective-permute-start.6) | collective-permute-done | bytes 36896 | tf_op jit(solution)/shard_map/ppermute | solution.py:390
  26.6 0.0 collective-permute-done.7.refs_3_
  26.6 0.0 copy-done.3
  26.6 0.0 copy-done.5
  26.6 0.0 copy-done.7
  26.6 0.9 %update.1 = (f32[8,128]{1,0:T(8,128)}, f32[8,128]{1,0:T(8,128)}, f32[8,128]{1,0:T(8,128)}) custom-call(f32[72,128]{1,0:T(8,128)S(1)} %get-tuple-element.20.refs_0_, f32[72,128]{1,0:T(8,128)S(1)} %collective-permute-done.5.refs_1_, f32[72,128]{1,0:T(8,128)S(1)} %collective-permute-done.6.refs_2_, f32[72,128]{1,0:T(8,128)S(1)} %collective-permute-done.7.refs_3_, ...), custom_call_target="tpu_custom_call" | custom-call | tf_op jit(solution)/shard_map/update/pallas_call | solution.py:394
Async XLA Ops:
  0.6 12.4 %collective-permute-start.1 = (f32[8,128]{1,0:T(8,128)}, f32[8,128]{1,0:T(8,128)S(1)}, u32[]{:S(2)}, u32[]{:S(2)}) collective-permute-start(f32[8,128]{1,0:T(8,128)} %bitcast.7), channel_id=1, source_target_pairs={{0,3},{1,2},{2,1},{3,0},{4,7},{5,6},{6,5},{7,4},{8,11},{9,10},{10,... | collective-permute-start | bytes 12296 | tf_op jit(solution)/shard_map/ppermute | solution.py:317
  3.1 9.9 %collective-permute-start = (f32[8,128]{1,0:T(8,128)}, f32[8,128]{1,0:T(8,128)S(1)}, u32[]{:S(2)}, u32[]{:S(2)}) collective-permute-start(f32[8,128]{1,0:T(8,128)} %bitcast.8), channel_id=1, source_target_pairs={{0,1},{1,0},{2,3},{3,2},{4,5},{5,4},{6,7},{7,6},{8,9},{9,8},{10,11... | collective-permute-start | bytes 12296 | tf_op jit(solution)/shard_map/ppermute | solution.py:316
  3.8 2.3 %copy-start = (f32[3,602,602]{2,1,0:T(8,128)S(1)}, f32[3,602,602]{2,1,0:T(8,128)}, u32[]{:S(2)}) copy-start(f32[3,602,602]{2,1,0:T(8,128)} %blocks_hbm.1) | copy-start | bytes 13046548
  6.1 0.7 %copy-start.1 = (f32[1024]{0:T(1024)S(1)}, f32[1024]{0:T(1024)}, u32[]{:S(2)}) copy-start(f32[1024]{0:T(1024)} %param.12) | copy-start | bytes 12292
  6.8 0.7 %copy-start.2 = (f32[1024]{0:T(1024)S(1)}, f32[1024]{0:T(1024)}, u32[]{:S(2)}) copy-start(f32[1024]{0:T(1024)} %param.11) | copy-start | bytes 12292
  7.5 0.7 %copy-start.4 = (f32[1024]{0:T(1024)S(1)}, f32[1024]{0:T(1024)}, u32[]{:S(2)}) copy-start(f32[1024]{0:T(1024)} %param.13) | copy-start | bytes 12292
  8.1 0.7 %copy-start.6 = (s32[3,602]{1,0:T(4,128)S(1)}, s32[3,602]{1,0:T(4,128)}, u32[]{:S(2)}) copy-start(s32[3,602]{1,0:T(4,128)} %dofs_ref.1) | copy-start | bytes 21676
  8.8 0.7 %copy-start.8 = (s32[1,256]{1,0:T(1,128)S(1)}, s32[1,256]{1,0:T(1,128)}, u32[]{:S(2)}) copy-start(s32[1,256]{1,0:T(1,128)} %left_ref.1) | copy-start | bytes 3076
  9.5 0.7 %copy-start.9 = (s32[1,256]{1,0:T(1,128)S(1)}, s32[1,256]{1,0:T(1,128)}, u32[]{:S(2)}) copy-start(s32[1,256]{1,0:T(1,128)} %right_ref.1) | copy-start | bytes 3076
  10.2 0.7 %copy-start.10 = (s32[3]{0:T(128)S(1)}, s32[3]{0:T(128)}, u32[]{:S(2)}) copy-start(s32[3]{0:T(128)} %order_ref.1) | copy-start | bytes 40
  10.9 0.7 %copy-start.11 = (s32[1,2]{1,0:T(1,128)S(1)}, s32[1,2]{1,0:T(1,128)}, u32[]{:S(2)}) copy-start(s32[1,2]{1,0:T(1,128)} %count_ref.1) | copy-start | bytes 28
  11.5 15.1 %copy-start.3 = (f32[1024]{0:T(1024)S(1)}, f32[1024]{0:T(1024)}, u32[]{:S(2)}) copy-start(f32[1024]{0:T(1024)} %param.11) | copy-start | bytes 12292
  11.5 15.1 %copy-start.5 = (f32[1024]{0:T(1024)S(1)}, f32[1024]{0:T(1024)}, u32[]{:S(2)}) copy-start(f32[1024]{0:T(1024)} %param.13) | copy-start | bytes 12292
  11.5 15.1 %copy-start.7 = (f32[1024]{0:T(1024)S(1)}, f32[1024]{0:T(1024)}, u32[]{:S(2)}) copy-start(f32[1024]{0:T(1024)} %param.10) | copy-start | bytes 12292
  14.3 3.7 %collective-permute-start.4 = (f32[72,128]{1,0:T(8,128)S(1)}, f32[72,128]{1,0:T(8,128)S(1)}, u32[]{:S(2)}, u32[]{:S(2)}) collective-permute-start(f32[72,128]{1,0:T(8,128)S(1)} %elements.1.refs_0_), channel_id=1, source_target_pairs={{0,3},{1,2},{2,1},{3,0},{4,7},{5,6},{6,5},{7,4},{8,11},{9,10},{10,... | collective-permute-start | bytes 110600 | tf_op jit(solution)/shard_map/ppermute | solution.py:358
  14.4 4.5 %collective-permute-start.3 = (f32[72,128]{1,0:T(8,128)S(1)}, f32[72,128]{1,0:T(8,128)S(1)}, u32[]{:S(2)}, u32[]{:S(2)}) collective-permute-start(f32[72,128]{1,0:T(8,128)S(1)} %elements.1.refs_0_), channel_id=1, source_target_pairs={{0,2},{1,3},{2,0},{3,1},{4,6},{5,7},{6,4},{7,5},{8,10},{9,11},{10,... | collective-permute-start | bytes 110600 | tf_op jit(solution)/shard_map/ppermute | solution.py:358
  16.0 2.9 %collective-permute-start.2 = (f32[72,128]{1,0:T(8,128)S(1)}, f32[72,128]{1,0:T(8,128)S(1)}, u32[]{:S(2)}, u32[]{:S(2)}) collective-permute-start(f32[72,128]{1,0:T(8,128)S(1)} %elements.1.refs_0_), channel_id=1, source_target_pairs={{0,1},{1,0},{2,3},{3,2},{4,5},{5,4},{6,7},{7,6},{8,9},{9,8},{10,11... | collective-permute-start | bytes 110600 | tf_op jit(solution)/shard_map/ppermute | solution.py:358
  19.1 4.3 %collective-permute-start.5 = (f32[72,128]{1,0:T(8,128)S(1)}, f32[72,128]{1,0:T(8,128)S(1)}, u32[]{:S(2)}, u32[]{:S(2)}) collective-permute-start(f32[72,128]{1,0:T(8,128)S(1)} %get-tuple-element.20.refs_0_), channel_id=1, source_target_pairs={{0,4},{1,9},{4,0},{5,13},{8,12},{9,1},{12,8},{13,5},{2,6},{3,11},{... | collective-permute-start | bytes 110600 | tf_op jit(solution)/shard_map/ppermute | solution.py:389
  20.8 5.8 %collective-permute-start.6 = (f32[72,128]{1,0:T(8,128)S(1)}, f32[72,128]{1,0:T(8,128)S(1)}, u32[]{:S(2)}, u32[]{:S(2)}) collective-permute-start(f32[72,128]{1,0:T(8,128)S(1)} %get-tuple-element.20.refs_0_), channel_id=1, source_target_pairs={{0,12},{1,13},{4,8},{5,9},{8,4},{9,5},{12,0},{13,1},{2,14},{3,15},... | collective-permute-start | bytes 110600 | tf_op jit(solution)/shard_map/ppermute | solution.py:390
  23.4 3.2 %collective-permute-start.7 = (f32[72,128]{1,0:T(8,128)S(1)}, f32[72,128]{1,0:T(8,128)S(1)}, u32[]{:S(2)}, u32[]{:S(2)}) collective-permute-start(f32[72,128]{1,0:T(8,128)S(1)} %collective-permute-done.5.refs_1_), channel_id=1, source_target_pairs={{0,1},{1,0},{2,3},{3,2},{4,5},{5,4},{6,7},{7,6},{8,9},{9,8},{10,11... | collective-permute-start | bytes 110600 | tf_op jit(solution)/shard_map/ppermute | solution.py:391

commit v3 on v2

--- a/solution.py
+++ b/solution.py
@@ -58,36 +58,53 @@
 
 def prepare_kernel(
     group_axes,
-    order_ref,
-    count_ref,
-    dofs_ref,
-    left_ref,
-    right_ref,
-    direction_ref,
-    residual_ref,
-    diagonal_ref,
-    blocks_hbm,
-    blocks_ref,
+    order_hbm,
+    count_hbm,
+    dofs_hbm,
+    left_hbm,
+    right_hbm,
+    solution_hbm,
+    residual_hbm,
+    direction_hbm,
+    diagonal_hbm,
     lane_ref,
     row_ref,
     pair_lane_ref,
     pair_row_ref,
     static_ref,
+    vector_ref,
+    dofs_ref,
     index_ref,
-    sem,
+    left_ref,
+    right_ref,
+    order_ref,
+    count_ref,
+    sems,
 ):
-    copy = pltpu.make_async_copy(blocks_hbm, blocks_ref, sem)
-    copy.start()
+    rows = direction_hbm.shape[0]
+    moves = [
+        (order_hbm, order_ref),
+        (count_hbm, count_ref),
+        (dofs_hbm, dofs_ref),
+        (left_hbm, left_ref),
+        (right_hbm, right_ref),
+    ]
+    for i, vector in enumerate((solution_hbm, residual_hbm, direction_hbm, diagonal_hbm)):
+        moves.append((vector, vector_ref.at[i * rows : (i + 1) * rows]))
+    copies = [pltpu.make_async_copy(*move, sems.at[i]) for i, move in enumerate(moves)]
+    for copy in copies:
+        copy.start()
     (outer, inner) = group_axes
     me = lax.axis_index(outer) * lax.axis_size(inner) + lax.axis_index(inner)
     elements, size = dofs_ref.shape
     width = index_ref.shape[1]
-    rows = direction_ref.shape[0]
     slot_bits = (rows * LANES - 1).bit_length()
     lane_bits = LANES.bit_length() - 1
     index_ref[...] = jnp.full(index_ref.shape, -1, jnp.int32)
+    lanes = lax.broadcasted_iota(jnp.int32, (1, width), 1)
+    for copy in copies:
+        copy.wait()
     index_ref[:elements, :size] = dofs_ref[...]
-    lanes = lax.broadcasted_iota(jnp.int32, (1, width), 1)
     for e in range(elements):
         order = order_ref[e]
         live = size * (6 * order * order + 2) // (6 * ORDER * ORDER + 2)
@@ -116,28 +133,30 @@
         preferred_element_type=jnp.float32,
     )
     owner = 1.0 - shared
-    direction = direction_ref[...]
-    diagonal = diagonal_ref[...]
-    scaled = diagonal * residual_ref[...]
+    residual = vector_ref[rows : 2 * rows]
+    direction = vector_ref[2 * rows : 3 * rows]
+    diagonal = vector_ref[3 * rows : 4 * rows]
+    scaled = diagonal * residual
     static_ref[0:8] = owner * diagonal
     static_ref[8:16] = owner * direction
     static_ref[16:24] = owner * scaled
-    static_ref[24:32] = owner * scaled * residual_ref[...]
+    static_ref[24:32] = owner * scaled * residual
     lines = []
     for table in (direction, scaled, diagonal):
         lines += as_rows(pick(table, pair_lane[:, :pairs], pair_row[:, :pairs]))
     lines += as_rows(slots.astype(jnp.float32))
     lines += [jnp.zeros((1, LANES), jnp.float32)] * (STATIC - 32 - len(lines))
     static_ref[32:STATIC] = jnp.concatenate(lines, axis=0)
-    copy.wait()
 
 
 def element_kernel(
-    own_ref, first_ref, second_ref, blocks_ref, lane_ref, row_ref, static_ref, out_ref, in_ref, y_ref
+    vector_ref, first_ref, second_ref, blocks_ref, lane_ref, row_ref, static_ref, out_ref, in_ref, y_ref
 ):
     elements, size, _ = blocks_ref.shape
     width = y_ref.shape[1]
-    window = jnp.concatenate([own_ref[...], first_ref[...], second_ref[...]], axis=0)
+    rows = first_ref.shape[0]
+    own = vector_ref[2 * rows : 3 * rows]
+    window = jnp.concatenate([own, first_ref[...], second_ref[...]], axis=0)
     element_in = pick(window, lane_ref[...], row_ref[...])
     in_ref[...] = jnp.zeros(in_ref.shape, jnp.float32)
     for e in range(elements):
@@ -206,10 +225,7 @@
         own_ref,
         pair_lane_ref,
         pair_row_ref,
-        solution_ref,
-        residual_ref,
-        direction_ref,
-        diagonal_ref,
+        vector_ref,
         new_solution_ref,
         new_residual_ref,
         new_direction_ref,
@@ -260,11 +276,13 @@
     old_norm = whole(old)
     step_size = old_norm / whole(curve)
     new_norm = whole(old - step_size * (2.0 * cross - step_size * square))
-    direction = direction_ref[...]
-    new_residual = residual_ref[...] - step_size * applied
-    new_solution_ref[...] = solution_ref[...] + step_size * direction
+    solution, residual, direction, diagonal = (
+        vector_ref[i * rows : (i + 1) * rows] for i in range(4)
+    )
+    new_residual = residual - step_size * applied
+    new_solution_ref[...] = solution + step_size * direction
     new_residual_ref[...] = new_residual
-    new_direction_ref[...] = diagonal_ref[...] * new_residual + (new_norm / old_norm) * direction
+    new_direction_ref[...] = diagonal * new_residual + (new_norm / old_norm) * direction
 
 
 def other_order(message, base, lines):
@@ -307,7 +325,7 @@
     lines = pairs // LANES
     rows = residual.shape[0] // LANES
     f32, bf16 = jnp.float32, jnp.bfloat16
-    vmem, smem = pltpu.VMEM, pltpu.SMEM
+    vmem = pltpu.VMEM
     params = pltpu.CompilerParams(vmem_limit_bytes=VMEM_LIMIT)
 
     solution, residual, direction, inverse_diagonal = (
@@ -316,31 +334,45 @@
     first = lax.ppermute(direction, group, swap_first(group_count))
     second = lax.ppermute(direction, group, swap_second(group_count))
 
-    blocks, lane_hot, row_hot, pair_lane, pair_row, static = pl.pallas_call(
+    lane_hot, row_hot, pair_lane, pair_row, static, vectors = pl.pallas_call(
         functools.partial(prepare_kernel, group),
         out_shape=[
-            jax.ShapeDtypeStruct(schur_blocks.shape, f32),
             jax.ShapeDtypeStruct((LANES, elements * width), bf16),
             jax.ShapeDtypeStruct((3 * rows, elements * width), f32),
             jax.ShapeDtypeStruct((LANES, 2 * pairs), bf16),
             jax.ShapeDtypeStruct((rows, 2 * pairs), f32),
             jax.ShapeDtypeStruct((STATIC, LANES), f32),
+            jax.ShapeDtypeStruct((4 * rows, LANES), f32),
         ],
-        in_specs=specs([smem, smem] + [vmem] * 6 + [pl.ANY]),
+        in_specs=specs([pltpu.HBM] * 9),
         out_specs=specs([vmem] * 6),
-        scratch_shapes=[pltpu.VMEM((8, width), jnp.int32), pltpu.SemaphoreType.DMA],
+        scratch_shapes=[
+            pltpu.VMEM((elements, size), jnp.int32),
+            pltpu.VMEM((8, width), jnp.int32),
+            pltpu.VMEM((1, pairs), jnp.int32),
+            pltpu.VMEM((1, pairs), jnp.int32),
+            pltpu.SMEM((elements,), jnp.int32),
+            pltpu.SMEM((1, 2), jnp.int32),
+            pltpu.SemaphoreType.DMA((9,)),
+        ],
         compiler_params=params,
+        cost_estimate=pl.CostEstimate(flops=1600000000, bytes_accessed=16000000, transcendentals=0),
         name="prepare",
     )(
-        element_order,
-        share_count,
-        elem_dofs,
-        left_slots,
-        right_slots,
-        direction,
-        residual,
-        inverse_diagonal,
-        schur_blocks,
+        *(
+            pltpu.with_memory_space_constraint(value, pltpu.HBM)
+            for value in (
+                element_order,
+                share_count,
+                elem_dofs,
+                left_slots,
+                right_slots,
+                solution,
+                residual,
+                direction,
+                inverse_diagonal,
+            )
+        )
     )
 
     message = pl.pallas_call(
@@ -351,7 +383,7 @@
         scratch_shapes=[pltpu.VMEM((8, width), f32), pltpu.VMEM((8, width), f32)],
         compiler_params=params,
         name="elements",
-    )(direction, first, second, blocks, lane_hot, row_hot, static)
+    )(vectors, first, second, schur_blocks, lane_hot, row_hot, static)
 
     if group_count == 4:
         messages = [message] + [
@@ -394,11 +426,11 @@
     outputs = pl.pallas_call(
         functools.partial(final_kernel, dom, "sub", ordered, dom_count, lines),
         out_shape=[jax.ShapeDtypeStruct((rows, LANES), f32)] * 3,
-        in_specs=specs([vmem] * (dom_count + 7)),
+        in_specs=specs([vmem] * (dom_count + 4)),
         out_specs=specs([vmem] * 3),
         compiler_params=params,
         name="update",
-    )(*messages, own, pair_lane, pair_row, solution, residual, direction, inverse_diagonal)
+    )(*messages, own, pair_lane, pair_row, vectors)
     return tuple(value.reshape(-1) for value in outputs)
 
 

time: 27.9 us -> 20.6 us (0.74)
  local copies, waits for them, and re-layouts: 7.76 us -> 0.01 us
  waiting for transfers between devices: 6.08 us -> 6.88 us
  Pallas kernels: 3.81 us -> 3.53 us
    unnamed x24 -> x2, local copies, waits for them, and re-layouts: 7.76 us -> 0.01 us
    ppermute x3, waiting for transfers between devices: 2.71 us -> 3.6 us  [local(): lax.ppermute(message, group, [(i, i ^ m) for i in range(4)])]
  transfers between devices with their start and end apart: 8 -> 8, of which waited for: 4 -> 3; matrix products, arithmetic and copies ran while one was open for 0% -> 0% of each run, Pallas kernels for 5% -> 6%
where the time goes in v3:
time: 20.6 us; the launch traced here: 20.4 us
  starting transfers between devices  9.31 us (45%)
  waiting for transfers between devices  6.88 us (33%)
  Pallas kernels  3.53 us (17%)
  between operations  0.69 us (3%)
    ppermute x3, waiting for transfers between devices, local(): lax.ppermute(message, group, [(i, i ^ m) for i in range(4)])  3.6 us
    ppermute x1, waiting for transfers between devices, local(): far = lax.ppermute(message, line, opposite)  3.27 us
    ppermute x1, starting transfers between devices, local(): far = lax.ppermute(message, line, opposite)  2.47 us
    ppermute x1, starting transfers between devices, local(): second = lax.ppermute(direction, group, swap_second(group_count))  2.44 us
    ppermute x3, starting transfers between devices, local(): lax.ppermute(message, group, [(i, i ^ m) for i in range(4)])  2.11 us
    ppermute x1, starting transfers between devices, local(): direct = lax.ppermute(message, line, near)  1.61 us
    pallas_call x1, Pallas kernels, local(): pl.pallas_call(element_kernel, out_shape=jax.ShapeDtypeStruct((SUMS + STA...  1.26 us
    pallas_call x1, Pallas kernels, local(): pl.pallas_call(functools.partial(prepare_kernel, group), out_shape=[jax.S...  1.2 us
  transfers between devices with their start and end apart: 8, of which 3 were waited for; matrix products, arithmetic and copies ran while one was open for 0% of the time, Pallas kernels for 6%

profile of v3, /device:TPU:0, one launch (start us, length us, event | category | flops | bytes accessed | tf_op | source)
XLA Modules:
  0.0 20.4 jit_solution(1024692265216197666)
XLA Ops:
  0.6 0.0 copy-start
  0.6 2.4 %collective-permute-start.1 = (f32[8,128]{1,0:T(8,128)}, f32[8,128]{1,0:T(8,128)S(1)}, u32[]{:S(2)}, u32[]{:S(2)}) collective-permute-start(f32[8,128]{1,0:T(8,128)} %bitcast.10), channel_id=1, source_target_pairs={{0,3},{1,2},{2,1},{3,0},{4,7},{5,6},{6,5},{7,4},{8,11},{9,10},{10,... | collective-permute-start | bytes 12296 | tf_op jit(solution)/shard_map/ppermute | solution.py:335
  3.1 0.7 %collective-permute-start = (f32[8,128]{1,0:T(8,128)}, f32[8,128]{1,0:T(8,128)S(1)}, u32[]{:S(2)}, u32[]{:S(2)}) collective-permute-start(f32[8,128]{1,0:T(8,128)} %bitcast.11), channel_id=1, source_target_pairs={{0,1},{1,0},{2,3},{3,2},{4,5},{5,4},{6,7},{7,6},{8,9},{9,8},{10,11... | collective-permute-start | bytes 12296 | tf_op jit(solution)/shard_map/ppermute | solution.py:334
  3.8 1.2 %prepare.1 = (bf16[128,1920]{1,0:T(8,128)(2,1)S(1)}, f32[24,1920]{1,0:T(8,128)S(1)}, bf16[128,512]{1,0:T(8,128)(2,1)S(1)}, f32[8,512]{1,0:T(8,128)S(1)}, f32[48,128]{1,0:T(8,128)S(1)}, /*index=5*/f32[32,128]{1,0:T(8,128)S(1)}) custom-call(s32[3]{0:T(128)} %order_hbm.1, s32[1,2]{1,0:T(1,128)} %count_hbm.1, s32[3,602]{1,0:T(4,128)} %dofs_hbm.1, ...), custom_call_target="tpu_custom_call" | custom-call | flops 1600000000 | bytes 16000000 | tf_op jit(solution)/shard_map/prepare/pallas_call | solution.py:337
  5.0 0.0 collective-permute-done.1.second_ref
  5.0 0.0 collective-permute-done.first_ref
  5.0 0.0 copy-done
  5.0 1.3 %elements.1.refs_0_ = f32[72,128]{1,0:T(8,128)S(1)} custom-call(f32[32,128]{1,0:T(8,128)S(1)} %get-tuple-element.14.vector_ref.refs_7_, f32[8,128]{1,0:T(8,128)S(1)} %collective-permute-done.first_ref, f32[8,128]{1,0:T(8,128)S(1)} %collective-permute-done.1.second_ref, f32[3,602,602]{2,1,0:T(8,128)S(1)} %copy-done, ...), custom_call_target="tpu_custom_call" | custom-call | tf_op jit(solution)/shard_map/elements/pallas_call | solution.py:378
  6.3 1.7 %collective-permute-start.4 = (f32[72,128]{1,0:T(8,128)S(1)}, f32[72,128]{1,0:T(8,128)S(1)}, u32[]{:S(2)}, u32[]{:S(2)}) collective-permute-start(f32[72,128]{1,0:T(8,128)S(1)} %elements.1.refs_0_), channel_id=1, source_target_pairs={{0,3},{1,2},{2,1},{3,0},{4,7},{5,6},{6,5},{7,4},{8,11},{9,10},{10,... | collective-permute-start | bytes 110600 | tf_op jit(solution)/shard_map/ppermute | solution.py:390
  8.0 0.4 %collective-permute-start.3 = (f32[72,128]{1,0:T(8,128)S(1)}, f32[72,128]{1,0:T(8,128)S(1)}, u32[]{:S(2)}, u32[]{:S(2)}) collective-permute-start(f32[72,128]{1,0:T(8,128)S(1)} %elements.1.refs_0_), channel_id=1, source_target_pairs={{0,2},{1,3},{2,0},{3,1},{4,6},{5,7},{6,4},{7,5},{8,10},{9,11},{10,... | collective-permute-start | bytes 110600 | tf_op jit(solution)/shard_map/ppermute | solution.py:390
  8.3 0.0 collective-permute-start.2
  8.4 1.5 %collective-permute-done.4.refs_3_ = f32[72,128]{1,0:T(8,128)S(1)} collective-permute-done((f32[72,128]{1,0:T(8,128)S(1)}, f32[72,128]{1,0:T(8,128)S(1)}, u32[]{:S(2)}, u32[]{:S(2)}) %collective-permute-start.4) | collective-permute-done | bytes 36896 | tf_op jit(solution)/shard_map/ppermute | solution.py:390
  9.8 2.1 %collective-permute-done.3.refs_2_ = f32[72,128]{1,0:T(8,128)S(1)} collective-permute-done((f32[72,128]{1,0:T(8,128)S(1)}, f32[72,128]{1,0:T(8,128)S(1)}, u32[]{:S(2)}, u32[]{:S(2)}) %collective-permute-start.3) | collective-permute-done | bytes 36896 | tf_op jit(solution)/shard_map/ppermute | solution.py:390
  12.0 0.0 collective-permute-done.2.refs_1_
  12.0 0.2 %sums.1 = (f32[8,128]{1,0:T(8,128)S(1)}, f32[72,128]{1,0:T(8,128)S(1)}) custom-call(f32[72,128]{1,0:T(8,128)S(1)} %elements.1.refs_0_, f32[72,128]{1,0:T(8,128)S(1)} %collective-permute-done.2.refs_1_, f32[72,128]{1,0:T(8,128)S(1)} %collective-permute-done.3.refs_2_, f32[72,128]{1,0:T(8,128)S(1)} %collective-permute-done.4.refs_3_, ...), custom_call_target="tpu_custom_call" | custom-call | tf_op jit(solution)/shard_map/sums/pallas_call | solution.py:401
  12.2 1.6 %collective-permute-start.5 = (f32[72,128]{1,0:T(8,128)S(1)}, f32[72,128]{1,0:T(8,128)S(1)}, u32[]{:S(2)}, u32[]{:S(2)}) collective-permute-start(f32[72,128]{1,0:T(8,128)S(1)} %get-tuple-element.20.refs_0_), channel_id=1, source_target_pairs={{0,4},{1,9},{4,0},{5,13},{8,12},{9,1},{12,8},{13,5},{2,6},{3,11},{... | collective-permute-start | bytes 110600 | tf_op jit(solution)/shard_map/ppermute | solution.py:421
  13.8 2.5 %collective-permute-start.6 = (f32[72,128]{1,0:T(8,128)S(1)}, f32[72,128]{1,0:T(8,128)S(1)}, u32[]{:S(2)}, u32[]{:S(2)}) collective-permute-start(f32[72,128]{1,0:T(8,128)S(1)} %get-tuple-element.20.refs_0_), channel_id=1, source_target_pairs={{0,12},{1,13},{4,8},{5,9},{8,4},{9,5},{12,0},{13,1},{2,14},{3,15},... | collective-permute-start | bytes 110600 | tf_op jit(solution)/shard_map/ppermute | solution.py:422
  16.3 0.0 collective-permute-done.5.refs_1_
  16.3 0.0 collective-permute-start.7
  16.3 3.3 %collective-permute-done.6.refs_2_ = f32[72,128]{1,0:T(8,128)S(1)} collective-permute-done((f32[72,128]{1,0:T(8,128)S(1)}, f32[72,128]{1,0:T(8,128)S(1)}, u32[]{:S(2)}, u32[]{:S(2)}) %collective-permute-start.6) | collective-permute-done | bytes 36896 | tf_op jit(solution)/shard_map/ppermute | solution.py:422
  19.6 0.0 collective-permute-done.7.refs_3_
  19.6 0.9 %update.1 = (f32[8,128]{1,0:T(8,128)}, f32[8,128]{1,0:T(8,128)}, f32[8,128]{1,0:T(8,128)}) custom-call(f32[72,128]{1,0:T(8,128)S(1)} %get-tuple-element.20.refs_0_, f32[72,128]{1,0:T(8,128)S(1)} %collective-permute-done.5.refs_1_, f32[72,128]{1,0:T(8,128)S(1)} %collective-permute-done.6.refs_2_, f32[72,128]{1,0:T(8,128)S(1)} %collective-permute-done.7.refs_3_, ...), custom_call_target="tpu_custom_call" | custom-call | tf_op jit(solution)/shard_map/update/pallas_call | solution.py:426
Async XLA Ops:
  0.6 4.4 %copy-start = (f32[3,602,602]{2,1,0:T(8,128)S(1)}, f32[3,602,602]{2,1,0:T(8,128)}, u32[]{:S(2)}) copy-start(f32[3,602,602]{2,1,0:T(8,128)} %blocks_ref.1) | copy-start | bytes 13046548
  0.6 4.3 %collective-permute-start.1 = (f32[8,128]{1,0:T(8,128)}, f32[8,128]{1,0:T(8,128)S(1)}, u32[]{:S(2)}, u32[]{:S(2)}) collective-permute-start(f32[8,128]{1,0:T(8,128)} %bitcast.10), channel_id=1, source_target_pairs={{0,3},{1,2},{2,1},{3,0},{4,7},{5,6},{6,5},{7,4},{8,11},{9,10},{10,... | collective-permute-start | bytes 12296 | tf_op jit(solution)/shard_map/ppermute | solution.py:335
  3.1 1.9 %collective-permute-start = (f32[8,128]{1,0:T(8,128)}, f32[8,128]{1,0:T(8,128)S(1)}, u32[]{:S(2)}, u32[]{:S(2)}) collective-permute-start(f32[8,128]{1,0:T(8,128)} %bitcast.11), channel_id=1, source_target_pairs={{0,1},{1,0},{2,3},{3,2},{4,5},{5,4},{6,7},{7,6},{8,9},{9,8},{10,11... | collective-permute-start | bytes 12296 | tf_op jit(solution)/shard_map/ppermute | solution.py:334
  6.3 3.6 %collective-permute-start.4 = (f32[72,128]{1,0:T(8,128)S(1)}, f32[72,128]{1,0:T(8,128)S(1)}, u32[]{:S(2)}, u32[]{:S(2)}) collective-permute-start(f32[72,128]{1,0:T(8,128)S(1)} %elements.1.refs_0_), channel_id=1, source_target_pairs={{0,3},{1,2},{2,1},{3,0},{4,7},{5,6},{6,5},{7,4},{8,11},{9,10},{10,... | collective-permute-start | bytes 110600 | tf_op jit(solution)/shard_map/ppermute | solution.py:390
  8.0 4.0 %collective-permute-start.3 = (f32[72,128]{1,0:T(8,128)S(1)}, f32[72,128]{1,0:T(8,128)S(1)}, u32[]{:S(2)}, u32[]{:S(2)}) collective-permute-start(f32[72,128]{1,0:T(8,128)S(1)} %elements.1.refs_0_), channel_id=1, source_target_pairs={{0,2},{1,3},{2,0},{3,1},{4,6},{5,7},{6,4},{7,5},{8,10},{9,11},{10,... | collective-permute-start | bytes 110600 | tf_op jit(solution)/shard_map/ppermute | solution.py:390
  8.3 3.6 %collective-permute-start.2 = (f32[72,128]{1,0:T(8,128)S(1)}, f32[72,128]{1,0:T(8,128)S(1)}, u32[]{:S(2)}, u32[]{:S(2)}) collective-permute-start(f32[72,128]{1,0:T(8,128)S(1)} %elements.1.refs_0_), channel_id=1, source_target_pairs={{0,1},{1,0},{2,3},{3,2},{4,5},{5,4},{6,7},{7,6},{8,9},{9,8},{10,11... | collective-permute-start | bytes 110600 | tf_op jit(solution)/shard_map/ppermute | solution.py:390
  12.2 4.1 %collective-permute-start.5 = (f32[72,128]{1,0:T(8,128)S(1)}, f32[72,128]{1,0:T(8,128)S(1)}, u32[]{:S(2)}, u32[]{:S(2)}) collective-permute-start(f32[72,128]{1,0:T(8,128)S(1)} %get-tuple-element.20.refs_0_), channel_id=1, source_target_pairs={{0,4},{1,9},{4,0},{5,13},{8,12},{9,1},{12,8},{13,5},{2,6},{3,11},{... | collective-permute-start | bytes 110600 | tf_op jit(solution)/shard_map/ppermute | solution.py:421
  13.8 5.8 %collective-permute-start.6 = (f32[72,128]{1,0:T(8,128)S(1)}, f32[72,128]{1,0:T(8,128)S(1)}, u32[]{:S(2)}, u32[]{:S(2)}) collective-permute-start(f32[72,128]{1,0:T(8,128)S(1)} %get-tuple-element.20.refs_0_), channel_id=1, source_target_pairs={{0,12},{1,13},{4,8},{5,9},{8,4},{9,5},{12,0},{13,1},{2,14},{3,15},... | collective-permute-start | bytes 110600 | tf_op jit(solution)/shard_map/ppermute | solution.py:422
  16.3 3.3 %collective-permute-start.7 = (f32[72,128]{1,0:T(8,128)S(1)}, f32[72,128]{1,0:T(8,128)S(1)}, u32[]{:S(2)}, u32[]{:S(2)}) collective-permute-start(f32[72,128]{1,0:T(8,128)S(1)} %collective-permute-done.5.refs_1_), channel_id=1, source_target_pairs={{0,1},{1,0},{2,3},{3,2},{4,5},{5,4},{6,7},{7,6},{8,9},{9,8},{10,11... | collective-permute-start | bytes 110600 | tf_op jit(solution)/shard_map/ppermute | solution.py:423

commit v4 on v3

--- a/solution.py
+++ b/solution.py
@@ -11,7 +11,9 @@
 LANES = 128
 VMEM_LIMIT = 32 * 1024 * 1024
 SUMS = 24
-STATIC = 48
+STATIC = 40
+SPLIT, BOTH = (2, 3), 1
+TOTALS = 8
 
 
 def split(value):
@@ -140,13 +142,12 @@
     static_ref[0:8] = owner * diagonal
     static_ref[8:16] = owner * direction
     static_ref[16:24] = owner * scaled
-    static_ref[24:32] = owner * scaled * residual
-    lines = []
+    lines = [jnp.sum(owner * scaled * residual, axis=0, keepdims=True)]
     for table in (direction, scaled, diagonal):
         lines += as_rows(pick(table, pair_lane[:, :pairs], pair_row[:, :pairs]))
     lines += as_rows(slots.astype(jnp.float32))
-    lines += [jnp.zeros((1, LANES), jnp.float32)] * (STATIC - 32 - len(lines))
-    static_ref[32:STATIC] = jnp.concatenate(lines, axis=0)
+    lines += [jnp.zeros((1, LANES), jnp.float32)] * (STATIC - 24 - len(lines))
+    static_ref[24:STATIC] = jnp.concatenate(lines, axis=0)
 
 
 def element_kernel(
@@ -183,16 +184,18 @@
     half_pairs = pair_lane_ref.shape[1] // 2
     lines = half_pairs // LANES
     lane_bits = LANES.bit_length() - 1
-    totals = [jnp.zeros((rows, LANES), jnp.float32) for _ in range(4)]
+    totals = [jnp.zeros((rows, LANES), jnp.float32) for _ in range(3)]
+    old = jnp.zeros((1, LANES), jnp.float32)
     found = [[] for _ in range(5)]
     for m, message in enumerate(messages):
         applied = message[0:8] + messages[m ^ 1][8:16] + messages[m ^ 3][16:24]
         at = functools.partial(lambda ref, i: ref[SUMS + 8 * i : SUMS + 8 * i + 8], message)
-        totals[0] += at(3)
-        totals[1] += at(1) * applied
-        totals[2] += at(2) * applied
-        totals[3] += at(0) * applied * applied
-        base = SUMS + 32
+        totals[0] += at(1) * applied
+        totals[1] += at(2) * applied
+        totals[2] += at(0) * applied * applied
+        base = SUMS + 24
+        old += message[base : base + 1]
+        base += 1
         if m == 0:
             own_ref[...] = applied
             pair_lane, pair_row = pair_lane_ref[...], pair_row_ref[...]
@@ -205,9 +208,10 @@
         found[1] += values[lines:]
         for i in range(3):
             found[2 + i].append(message[base + i * lines : base + (i + 1) * lines])
-    for i in range(4):
-        out_ref[i * rows : (i + 1) * rows] = totals[i]
-    base, step = 4 * rows, count * lines
+    heads = [old] + [jnp.sum(total, axis=0, keepdims=True) for total in totals]
+    heads.append(jnp.zeros((TOTALS - len(heads), LANES), jnp.float32))
+    out_ref[:TOTALS] = jnp.concatenate(heads, axis=0)
+    base, step = TOTALS, count * lines
     for i in range(5):
         out_ref[base + i * step : base + (i + 1) * step] = jnp.concatenate(found[i], axis=0)
 
@@ -234,19 +238,22 @@
     me = lax.axis_index(dom_axis)
     if not ordered:
         own, direct, far, relayed = messages
-        relayed = other_order(relayed, 4 * rows, lines)
+        far, relayed = (other_order(value, TOTALS, lines) for value in (far, relayed))
         even = lax.axis_index(inner_axis) == 0
-        line = [own, jnp.where(even, direct, relayed), jnp.where(even, relayed, direct), far]
+        line = [own] + [None] * 3
+        line[SPLIT[0]] = jnp.where(even, direct, relayed)
+        line[SPLIT[1]] = jnp.where(even, relayed, direct)
+        line[BOTH] = far
         low = (me & 1) == 0
         high = (me & 2) == 0
         line = [jnp.where(low, line[i], line[i ^ 1]) for i in range(4)]
         messages = [jnp.where(high, line[i], line[i ^ 2]) for i in range(4)]
-    base = 4 * rows
+    base = TOTALS
     step = (messages[0].shape[0] - base) // 5
     totals = messages[0][:base]
     for message in messages[1:]:
         totals = totals + message[:base]
-    old, curve, cross, square = (totals[i * rows : (i + 1) * rows] for i in range(4))
+    terms = [jnp.zeros((step, LANES), jnp.float32) for _ in range(3)]
 
     def part(message, i):
         return message[base + i * step : base + (i + 1) * step]
@@ -256,23 +263,21 @@
     for d in range(count - 1):
         near, next_one = messages[d], messages[d + 1]
         forward, backward = part(near, 0), part(next_one, 1)
-        terms = [
-            part(near, 2) * backward,
-            part(near, 3) * backward,
-            part(near, 4) * backward * (2.0 * forward + backward),
-        ]
-        for start in range(0, step, rows):
-            curve = curve + terms[0][start : start + rows]
-            cross = cross + terms[1][start : start + rows]
-            square = square + terms[2][start : start + rows]
+        terms[0] += part(near, 2) * backward
+        terms[1] += part(near, 3) * backward
+        terms[2] += part(near, 4) * backward * (2.0 * forward + backward)
         from_left = jnp.where(me == d + 1, forward[:lines], from_left)
         from_right = jnp.where(me == d, backward[:lines], from_right)
     incoming = as_row(jnp.concatenate([from_right, from_left], axis=0))
     applied = own_ref[...] + place(incoming, pair_lane_ref[...], pair_row_ref[...])
 
     def whole(value):
-        return jnp.sum(value, axis=(0, 1), keepdims=True)
-
+        return jnp.sum(value, axis=1, keepdims=True)
+
+    old = totals[0:1]
+    curve, cross, square = (
+        totals[i + 1 : i + 2] + jnp.sum(terms[i], axis=0, keepdims=True) for i in range(3)
+    )
     old_norm = whole(old)
     step_size = old_norm / whole(curve)
     new_norm = whole(old - step_size * (2.0 * cross - step_size * square))
@@ -386,9 +391,10 @@
     )(vectors, first, second, schur_blocks, lane_hot, row_hot, static)
 
     if group_count == 4:
-        messages = [message] + [
-            lax.ppermute(message, group, [(i, i ^ m) for i in range(4)]) for m in (1, 2, 3)
-        ]
+        first = lax.ppermute(message, group, swap_first(group_count))
+        second = lax.ppermute(message, group, swap_second(group_count))
+        relayed = lax.ppermute(second, group, swap_first(group_count))
+        messages = [message, first, relayed, second]
     else:
         me = lax.axis_index(group)
         order = me ^ jnp.arange(group_count)
@@ -402,7 +408,7 @@
         functools.partial(sum_kernel, group_count),
         out_shape=[
             jax.ShapeDtypeStruct((rows, LANES), f32),
-            jax.ShapeDtypeStruct((4 * rows + 5 * group_count * lines, LANES), f32),
+            jax.ShapeDtypeStruct((TOTALS + 5 * group_count * lines, LANES), f32),
         ],
         in_specs=specs([vmem] * (group_count + 2)),
         out_specs=specs([vmem] * 2),
@@ -416,10 +422,10 @@
         messages = [everyone[d] for d in range(dom_count)]
     else:
         line = (dom, "sub")
-        near = [(2 * d + s, 2 * (d ^ (1 + s)) + s) for d in range(4) for s in range(2)]
-        opposite = [(2 * d + s, 2 * (d ^ 3) + s) for d in range(4) for s in range(2)]
-        direct = lax.ppermute(message, line, near)
-        far = lax.ppermute(message, line, opposite)
+        split = [(2 * d + s, 2 * (d ^ SPLIT[s]) + s) for d in range(4) for s in range(2)]
+        both = [(2 * d + s, 2 * (d ^ BOTH) + 1 - s) for d in range(4) for s in range(2)]
+        direct = lax.ppermute(message, line, split)
+        far = lax.ppermute(message, line, both)
         relayed = lax.ppermute(direct, "sub", [(0, 1), (1, 0)])
         messages = [message, direct, far, relayed]
 

time: 20.6 us -> 18.9 us (0.917)
  the two profiles are of different devices: /device:TPU:0 before, /device:TPU:1 now
where the time goes in v4:
time: 18.9 us; the launch traced here: 18.7 us
  starting transfers between devices  9.54 us (50%)
  waiting for transfers between devices  5.03 us (27%)
  Pallas kernels  3.44 us (18%)
  between operations  0.67 us (4%)
    ppermute x1, starting transfers between devices, local(): direct = lax.ppermute(message, line, split)  3.71 us
    ppermute x1, starting transfers between devices, local(): second = lax.ppermute(direction, group, swap_second(group_count))  2.67 us
    ppermute x1, starting transfers between devices, local(): second = lax.ppermute(message, group, swap_second(group_count))  1.83 us
    ppermute x1, waiting for transfers between devices, local(): far = lax.ppermute(message, line, both)  1.83 us
    ppermute x1, waiting for transfers between devices, local(): second = lax.ppermute(message, group, swap_second(group_count))  1.48 us
    pallas_call x1, Pallas kernels, local(): pl.pallas_call(functools.partial(prepare_kernel, group), out_shape=[jax.S...  1.2 us
    pallas_call x1, Pallas kernels, local(): pl.pallas_call(element_kernel, out_shape=jax.ShapeDtypeStruct((SUMS + STA...  1.17 us
    ppermute x1, waiting for transfers between devices, local(): relayed = lax.ppermute(second, group, swap_first(group_count))  1 us
  transfers between devices with their start and end apart: 8, of which 5 were waited for; matrix products, arithmetic and copies ran while one was open for 0% of the time, Pallas kernels for 6%

profile of v4, /device:TPU:1, one launch (start us, length us, event | category | flops | bytes accessed | tf_op | source)
XLA Modules:
  0.0 18.7 jit_solution(4626837375353291871)
XLA Ops:
  0.6 0.0 copy-start
  0.6 2.7 %collective-permute-start.1 = (f32[8,128]{1,0:T(8,128)}, f32[8,128]{1,0:T(8,128)S(1)}, u32[]{:S(2)}, u32[]{:S(2)}) collective-permute-start(f32[8,128]{1,0:T(8,128)} %bitcast.10), channel_id=1, source_target_pairs={{0,3},{1,2},{2,1},{3,0},{4,7},{5,6},{6,5},{7,4},{8,11},{9,10},{10,... | collective-permute-start | bytes 12296 | tf_op jit(solution)/shard_map/ppermute | solution.py:340
  3.3 0.0 collective-permute-start
  3.3 1.2 %prepare.1 = (bf16[128,1920]{1,0:T(8,128)(2,1)S(1)}, f32[24,1920]{1,0:T(8,128)S(1)}, bf16[128,512]{1,0:T(8,128)(2,1)S(1)}, f32[8,512]{1,0:T(8,128)S(1)}, f32[40,128]{1,0:T(8,128)S(1)}, /*index=5*/f32[32,128]{1,0:T(8,128)S(1)}) custom-call(s32[3]{0:T(128)} %order_hbm.1, s32[1,2]{1,0:T(1,128)} %count_hbm.1, s32[3,602]{1,0:T(4,128)} %dofs_hbm.1, ...), custom_call_target="tpu_custom_call" | custom-call | flops 1600000000 | bytes 16000000 | tf_op jit(solution)/shard_map/prepare/pallas_call | solution.py:342
  4.5 0.3 %collective-permute-done.1.second_ref = f32[8,128]{1,0:T(8,128)S(1)} collective-permute-done((f32[8,128]{1,0:T(8,128)}, f32[8,128]{1,0:T(8,128)S(1)}, u32[]{:S(2)}, u32[]{:S(2)}) %collective-permute-start.1) | collective-permute-done | bytes 4128 | tf_op jit(solution)/shard_map/ppermute | solution.py:340
  4.8 0.0 collective-permute-done.first_ref
  4.8 0.0 copy-done
  4.8 1.2 %elements.1.refs_0_ = f32[64,128]{1,0:T(8,128)S(1)} custom-call(f32[32,128]{1,0:T(8,128)S(1)} %get-tuple-element.14.vector_ref.refs_7_, f32[8,128]{1,0:T(8,128)S(1)} %collective-permute-done.first_ref, f32[8,128]{1,0:T(8,128)S(1)} %collective-permute-done.1.second_ref, f32[3,602,602]{2,1,0:T(8,128)S(1)} %copy-done, ...), custom_call_target="tpu_custom_call" | custom-call | tf_op jit(solution)/shard_map/elements/pallas_call | solution.py:383
  6.0 1.8 %collective-permute-start.3 = (f32[64,128]{1,0:T(8,128)S(1)}, f32[64,128]{1,0:T(8,128)S(1)}, u32[]{:S(2)}, u32[]{:S(2)}) collective-permute-start(f32[64,128]{1,0:T(8,128)S(1)} %elements.1.refs_0_), channel_id=1, source_target_pairs={{0,3},{1,2},{2,1},{3,0},{4,7},{5,6},{6,5},{7,4},{8,11},{9,10},{10,... | collective-permute-start | bytes 98312 | tf_op jit(solution)/shard_map/ppermute | solution.py:395
  7.8 0.1 collective-permute-start.2
  7.9 1.5 %collective-permute-done.3.refs_3_ = f32[64,128]{1,0:T(8,128)S(1)} collective-permute-done((f32[64,128]{1,0:T(8,128)S(1)}, f32[64,128]{1,0:T(8,128)S(1)}, u32[]{:S(2)}, u32[]{:S(2)}) %collective-permute-start.3) | collective-permute-done | bytes 32800 | tf_op jit(solution)/shard_map/ppermute | solution.py:395
  9.4 0.2 %collective-permute-start.4 = (f32[64,128]{1,0:T(8,128)S(1)}, f32[64,128]{1,0:T(8,128)S(1)}, u32[]{:S(2)}, u32[]{:S(2)}) collective-permute-start(f32[64,128]{1,0:T(8,128)S(1)} %collective-permute-done.3.refs_3_), channel_id=1, source_target_pairs={{0,1},{1,0},{2,3},{3,2},{4,5},{5,4},{6,7},{7,6},{8,9},{9,8},{10,11... | collective-permute-start | bytes 98312 | tf_op jit(solution)/shard_map/ppermute | solution.py:396
  9.6 0.0 collective-permute-done.2.refs_1_
  9.6 1.0 %collective-permute-done.4.refs_2_ = f32[64,128]{1,0:T(8,128)S(1)} collective-permute-done((f32[64,128]{1,0:T(8,128)S(1)}, f32[64,128]{1,0:T(8,128)S(1)}, u32[]{:S(2)}, u32[]{:S(2)}) %collective-permute-start.4) | collective-permute-done | bytes 32800 | tf_op jit(solution)/shard_map/ppermute | solution.py:396
  10.6 0.2 %sums.1 = (f32[8,128]{1,0:T(8,128)S(1)}, f32[48,128]{1,0:T(8,128)S(1)}) custom-call(f32[64,128]{1,0:T(8,128)S(1)} %elements.1.refs_0_, f32[64,128]{1,0:T(8,128)S(1)} %collective-permute-done.2.refs_1_, f32[64,128]{1,0:T(8,128)S(1)} %collective-permute-done.4.refs_2_, f32[64,128]{1,0:T(8,128)S(1)} %collective-permute-done.3.refs_3_, ...), custom_call_target="tpu_custom_call" | custom-call | tf_op jit(solution)/shard_map/sums/pallas_call | solution.py:407
  10.9 3.7 %collective-permute-start.5 = (f32[48,128]{1,0:T(8,128)S(1)}, f32[48,128]{1,0:T(8,128)S(1)}, u32[]{:S(2)}, u32[]{:S(2)}) collective-permute-start(f32[48,128]{1,0:T(8,128)S(1)} %get-tuple-element.20.refs_0_), channel_id=1, source_target_pairs={{0,8},{1,13},{4,12},{5,9},{8,0},{9,5},{12,4},{13,1},{2,10},{3,15},... | collective-permute-start | bytes 73736 | tf_op jit(solution)/shard_map/ppermute | solution.py:427
  14.6 0.8 %collective-permute-start.6 = (f32[48,128]{1,0:T(8,128)S(1)}, f32[48,128]{1,0:T(8,128)S(1)}, u32[]{:S(2)}, u32[]{:S(2)}) collective-permute-start(f32[48,128]{1,0:T(8,128)S(1)} %get-tuple-element.20.refs_0_), channel_id=1, source_target_pairs={{0,5},{1,4},{4,1},{5,0},{8,13},{9,12},{12,9},{13,8},{2,7},{3,6},{6... | collective-permute-start | bytes 73736 | tf_op jit(solution)/shard_map/ppermute | solution.py:428
  15.4 0.4 %collective-permute-done.5.refs_1_ = f32[48,128]{1,0:T(8,128)S(1)} collective-permute-done((f32[48,128]{1,0:T(8,128)S(1)}, f32[48,128]{1,0:T(8,128)S(1)}, u32[]{:S(2)}, u32[]{:S(2)}) %collective-permute-start.5) | collective-permute-done | bytes 24608 | tf_op jit(solution)/shard_map/ppermute | solution.py:427
  15.8 0.2 %collective-permute-start.7 = (f32[48,128]{1,0:T(8,128)S(1)}, f32[48,128]{1,0:T(8,128)S(1)}, u32[]{:S(2)}, u32[]{:S(2)}) collective-permute-start(f32[48,128]{1,0:T(8,128)S(1)} %collective-permute-done.5.refs_1_), channel_id=1, source_target_pairs={{0,1},{1,0},{2,3},{3,2},{4,5},{5,4},{6,7},{7,6},{8,9},{9,8},{10,11... | collective-permute-start | bytes 73736 | tf_op jit(solution)/shard_map/ppermute | solution.py:429
  16.0 1.8 %collective-permute-done.6.refs_2_ = f32[48,128]{1,0:T(8,128)S(1)} collective-permute-done((f32[48,128]{1,0:T(8,128)S(1)}, f32[48,128]{1,0:T(8,128)S(1)}, u32[]{:S(2)}, u32[]{:S(2)}) %collective-permute-start.6) | collective-permute-done | bytes 24608 | tf_op jit(solution)/shard_map/ppermute | solution.py:428
  17.8 0.0 collective-permute-done.7.refs_3_
  17.8 0.9 %update.1 = (f32[8,128]{1,0:T(8,128)}, f32[8,128]{1,0:T(8,128)}, f32[8,128]{1,0:T(8,128)}) custom-call(f32[48,128]{1,0:T(8,128)S(1)} %get-tuple-element.20.refs_0_, f32[48,128]{1,0:T(8,128)S(1)} %collective-permute-done.5.refs_1_, f32[48,128]{1,0:T(8,128)S(1)} %collective-permute-done.6.refs_2_, f32[48,128]{1,0:T(8,128)S(1)} %collective-permute-done.7.refs_3_, ...), custom_call_target="tpu_custom_call" | custom-call | tf_op jit(solution)/shard_map/update/pallas_call | solution.py:432
Async XLA Ops:
  0.6 4.2 %copy-start = (f32[3,602,602]{2,1,0:T(8,128)S(1)}, f32[3,602,602]{2,1,0:T(8,128)}, u32[]{:S(2)}) copy-start(f32[3,602,602]{2,1,0:T(8,128)} %blocks_ref.1) | copy-start | bytes 13046548
  0.6 4.2 %collective-permute-start.1 = (f32[8,128]{1,0:T(8,128)}, f32[8,128]{1,0:T(8,128)S(1)}, u32[]{:S(2)}, u32[]{:S(2)}) collective-permute-start(f32[8,128]{1,0:T(8,128)} %bitcast.10), channel_id=1, source_target_pairs={{0,3},{1,2},{2,1},{3,0},{4,7},{5,6},{6,5},{7,4},{8,11},{9,10},{10,... | collective-permute-start | bytes 12296 | tf_op jit(solution)/shard_map/ppermute | solution.py:340
  3.3 1.5 %collective-permute-start = (f32[8,128]{1,0:T(8,128)}, f32[8,128]{1,0:T(8,128)S(1)}, u32[]{:S(2)}, u32[]{:S(2)}) collective-permute-start(f32[8,128]{1,0:T(8,128)} %bitcast.11), channel_id=1, source_target_pairs={{0,1},{1,0},{2,3},{3,2},{4,5},{5,4},{6,7},{7,6},{8,9},{9,8},{10,11... | collective-permute-start | bytes 12296 | tf_op jit(solution)/shard_map/ppermute | solution.py:339
  6.0 3.4 %collective-permute-start.3 = (f32[64,128]{1,0:T(8,128)S(1)}, f32[64,128]{1,0:T(8,128)S(1)}, u32[]{:S(2)}, u32[]{:S(2)}) collective-permute-start(f32[64,128]{1,0:T(8,128)S(1)} %elements.1.refs_0_), channel_id=1, source_target_pairs={{0,3},{1,2},{2,1},{3,0},{4,7},{5,6},{6,5},{7,4},{8,11},{9,10},{10,... | collective-permute-start | bytes 98312 | tf_op jit(solution)/shard_map/ppermute | solution.py:395
  7.8 1.8 %collective-permute-start.2 = (f32[64,128]{1,0:T(8,128)S(1)}, f32[64,128]{1,0:T(8,128)S(1)}, u32[]{:S(2)}, u32[]{:S(2)}) collective-permute-start(f32[64,128]{1,0:T(8,128)S(1)} %elements.1.refs_0_), channel_id=1, source_target_pairs={{0,1},{1,0},{2,3},{3,2},{4,5},{5,4},{6,7},{7,6},{8,9},{9,8},{10,11... | collective-permute-start | bytes 98312 | tf_op jit(solution)/shard_map/ppermute | solution.py:394
  9.4 1.2 %collective-permute-start.4 = (f32[64,128]{1,0:T(8,128)S(1)}, f32[64,128]{1,0:T(8,128)S(1)}, u32[]{:S(2)}, u32[]{:S(2)}) collective-permute-start(f32[64,128]{1,0:T(8,128)S(1)} %collective-permute-done.3.refs_3_), channel_id=1, source_target_pairs={{0,1},{1,0},{2,3},{3,2},{4,5},{5,4},{6,7},{7,6},{8,9},{9,8},{10,11... | collective-permute-start | bytes 98312 | tf_op jit(solution)/shard_map/ppermute | solution.py:396
  10.9 4.9 %collective-permute-start.5 = (f32[48,128]{1,0:T(8,128)S(1)}, f32[48,128]{1,0:T(8,128)S(1)}, u32[]{:S(2)}, u32[]{:S(2)}) collective-permute-start(f32[48,128]{1,0:T(8,128)S(1)} %get-tuple-element.20.refs_0_), channel_id=1, source_target_pairs={{0,8},{1,13},{4,12},{5,9},{8,0},{9,5},{12,4},{13,1},{2,10},{3,15},... | collective-permute-start | bytes 73736 | tf_op jit(solution)/shard_map/ppermute | solution.py:427
  14.6 3.3 %collective-permute-start.6 = (f32[48,128]{1,0:T(8,128)S(1)}, f32[48,128]{1,0:T(8,128)S(1)}, u32[]{:S(2)}, u32[]{:S(2)}) collective-permute-start(f32[48,128]{1,0:T(8,128)S(1)} %get-tuple-element.20.refs_0_), channel_id=1, source_target_pairs={{0,5},{1,4},{4,1},{5,0},{8,13},{9,12},{12,9},{13,8},{2,7},{3,6},{6... | collective-permute-start | bytes 73736 | tf_op jit(solution)/shard_map/ppermute | solution.py:428
  15.8 2.0 %collective-permute-start.7 = (f32[48,128]{1,0:T(8,128)S(1)}, f32[48,128]{1,0:T(8,128)S(1)}, u32[]{:S(2)}, u32[]{:S(2)}) collective-permute-start(f32[48,128]{1,0:T(8,128)S(1)} %collective-permute-done.5.refs_1_), channel_id=1, source_target_pairs={{0,1},{1,0},{2,3},{3,2},{4,5},{5,4},{6,7},{7,6},{8,9},{9,8},{10,11... | collective-permute-start | bytes 73736 | tf_op jit(solution)/shard_map/ppermute | solution.py:429

commit v5 on v4

--- a/solution.py
+++ b/solution.py
@@ -27,13 +27,17 @@
     return value.astype(jnp.bfloat16)
 
 
-def pick(table, lane_hot, row_hot):
-    rows = table.shape[0]
-    parts = jnp.dot(
-        half(jnp.concatenate(split(table), axis=0)), lane_hot, preferred_element_type=jnp.float32
-    )
-    found = (parts[:rows] + parts[rows : 2 * rows]) + parts[2 * rows :]
-    return jnp.sum(found * row_hot, axis=0, keepdims=True)
+def look_up(table, low, high):
+    found = jnp.zeros(low.shape, jnp.float32)
+    for row in range(table.shape[0]):
+        line = jnp.broadcast_to(table[row : row + 1], low.shape)
+        line = jnp.take_along_axis(line, low, axis=1, mode="promise_in_bounds")
+        found = jnp.where(high == row, line, found)
+    return found
+
+
+def lanes_of(slots):
+    return slots & (LANES - 1), lax.shift_right_arithmetic(slots, LANES.bit_length() - 1)
 
 
 def place(values, lane_hot, row_hot):
@@ -52,10 +56,6 @@
 
 def as_rows(row):
     return [row[:, i * LANES : (i + 1) * LANES] for i in range(row.shape[1] // LANES)]
-
-
-def as_row(rows):
-    return jnp.concatenate([rows[i : i + 1] for i in range(rows.shape[0])], axis=1)
 
 
 def prepare_kernel(
@@ -71,12 +71,11 @@
     diagonal_hbm,
     lane_ref,
     row_ref,
-    pair_lane_ref,
-    pair_row_ref,
+    index_ref,
     static_ref,
     vector_ref,
     dofs_ref,
-    index_ref,
+    wide_ref,
     left_ref,
     right_ref,
     order_ref,
@@ -99,42 +98,62 @@
     (outer, inner) = group_axes
     me = lax.axis_index(outer) * lax.axis_size(inner) + lax.axis_index(inner)
     elements, size = dofs_ref.shape
-    width = index_ref.shape[1]
+    width = wide_ref.shape[1]
     slot_bits = (rows * LANES - 1).bit_length()
-    lane_bits = LANES.bit_length() - 1
-    index_ref[...] = jnp.full(index_ref.shape, -1, jnp.int32)
+    wide_ref[...] = jnp.zeros(wide_ref.shape, jnp.int32)
     lanes = lax.broadcasted_iota(jnp.int32, (1, width), 1)
+    eighth = lax.broadcasted_iota(jnp.int32, (8, width), 0) == (
+        lax.broadcasted_iota(jnp.int32, (8, width), 1) & 7
+    )
+    tile = jnp.where(
+        lax.shift_right_logical(lax.broadcasted_iota(jnp.int32, (width, LANES), 0), 3)
+        == lax.broadcasted_iota(jnp.int32, (width, LANES), 1),
+        1.0,
+        0.0,
+    )
     for copy in copies:
         copy.wait()
-    index_ref[:elements, :size] = dofs_ref[...]
+    wide_ref[:elements, :size] = dofs_ref[...]
+    parts = []
     for e in range(elements):
         order = order_ref[e]
         live = size * (6 * order * order + 2) // (6 * ORDER * ORDER + 2)
         active = lanes < live
-        dofs = index_ref[e : e + 1, :]
+        dofs = wide_ref[e : e + 1, :]
         piece = lax.shift_right_logical(dofs, slot_bits)
         place_of = jnp.where(piece == me, 0, jnp.where(piece == (me ^ 1), 1, 2))
-        high = place_of * rows + (lax.shift_right_logical(dofs, lane_bits) & (rows - 1))
-        low = jnp.where(active, dofs & (LANES - 1), -1)
+        low, high = lanes_of(dofs)
+        high = place_of * rows + (high & (rows - 1))
+        low = jnp.where(active, low, -1)
         high = jnp.where(active, high, -1)
         lane_ref[:, e * width : (e + 1) * width] = half(hot(low, LANES))
         row_ref[:, e * width : (e + 1) * width] = hot(high, 3 * rows)
+        for value in (low, high):
+            parts.append(jnp.where(eighth, (value + 1).astype(jnp.float32), 0.0))
+    packed = jnp.dot(
+        half(jnp.concatenate(parts, axis=0)), half(tile), preferred_element_type=jnp.float32
+    )
+    packed = packed.astype(jnp.int32) - 1
+    for e in range(elements):
+        index_ref[16 * e : 16 * e + 8] = jnp.maximum(packed[16 * e : 16 * e + 8], 0)
+        index_ref[16 * e + 8 : 16 * e + 16] = packed[16 * e + 8 : 16 * e + 16]
     pairs = left_ref.shape[1]
     pair_lanes = lax.broadcasted_iota(jnp.int32, (1, pairs), 1)
     right = jnp.where(pair_lanes < count_ref[0, 1], right_ref[...], -1)
     left = jnp.where(pair_lanes < count_ref[0, 0], left_ref[...], -1)
     slots = jnp.concatenate([right, left], axis=1)
-    pair_lane = half(hot(jnp.where(slots < 0, -1, slots & (LANES - 1)), LANES))
-    pair_row = hot(lax.shift_right_arithmetic(slots, lane_bits), rows)
-    pair_lane_ref[...] = pair_lane
-    pair_row_ref[...] = pair_row
-    shared = lax.dot_general(
-        half(pair_row[:, pairs:]),
-        pair_lane[:, pairs:],
-        (((1,), (1,)), ((), ())),
-        preferred_element_type=jnp.float32,
-    )
-    owner = 1.0 - shared
+    low, high = lanes_of(slots)
+    position = lax.broadcasted_iota(jnp.int32, slots.shape, 1)
+    source = place(
+        (position + 1).astype(jnp.float32),
+        half(hot(jnp.where(slots < 0, -1, low), LANES)),
+        hot(high, rows),
+    )
+    source = source.astype(jnp.int32) - 1
+    low, high = lanes_of(source)
+    index_ref[16 * elements : 16 * elements + 8] = low
+    index_ref[16 * elements + 8 : 16 * elements + 16] = high
+    owner = jnp.where(source >= pairs, 0.0, 1.0)
     residual = vector_ref[rows : 2 * rows]
     direction = vector_ref[2 * rows : 3 * rows]
     diagonal = vector_ref[3 * rows : 4 * rows]
@@ -142,48 +161,56 @@
     static_ref[0:8] = owner * diagonal
     static_ref[8:16] = owner * direction
     static_ref[16:24] = owner * scaled
-    lines = [jnp.sum(owner * scaled * residual, axis=0, keepdims=True)]
+    lists = as_rows(slots)
+    count = len(lists)
+    lists = jnp.concatenate(lists + [jnp.full((8 - count, LANES), -1, jnp.int32)], axis=0)
+    lines = [lists[:count].astype(jnp.float32)]
+    lines.append(jnp.sum(owner * scaled * residual, axis=0, keepdims=True))
     for table in (direction, scaled, diagonal):
-        lines += as_rows(pick(table, pair_lane[:, :pairs], pair_row[:, :pairs]))
-    lines += as_rows(slots.astype(jnp.float32))
-    lines += [jnp.zeros((1, LANES), jnp.float32)] * (STATIC - 24 - len(lines))
+        lines.append(look_up(table, *lanes_of(lists))[: count // 2])
+    used = 24 + count + 1 + 3 * (count // 2)
+    lines.append(jnp.zeros((STATIC - used, LANES), jnp.float32))
     static_ref[24:STATIC] = jnp.concatenate(lines, axis=0)
 
 
 def element_kernel(
-    vector_ref, first_ref, second_ref, blocks_ref, lane_ref, row_ref, static_ref, out_ref, in_ref, y_ref
+    vector_ref, first_ref, second_ref, blocks_ref, lane_ref, row_ref, index_ref, static_ref, out_ref
 ):
     elements, size, _ = blocks_ref.shape
-    width = y_ref.shape[1]
+    width = lane_ref.shape[1] // elements
     rows = first_ref.shape[0]
-    own = vector_ref[2 * rows : 3 * rows]
-    window = jnp.concatenate([own, first_ref[...], second_ref[...]], axis=0)
-    element_in = pick(window, lane_ref[...], row_ref[...])
-    in_ref[...] = jnp.zeros(in_ref.shape, jnp.float32)
+    window = jnp.concatenate(
+        [vector_ref[2 * rows : 3 * rows], first_ref[...], second_ref[...]], axis=0
+    )
+    whole = size // 8 * 8
+    sums = None
     for e in range(elements):
-        in_ref[e : e + 1, :] = element_in[:, e * width : (e + 1) * width]
-    columns = in_ref[...].T
-    y_ref[...] = jnp.zeros(y_ref.shape, jnp.float32)
-    whole = size // 8 * 8
-    for e in range(elements):
+        low, high = index_ref[16 * e : 16 * e + 8], index_ref[16 * e + 8 : 16 * e + 16]
+        element_in = look_up(window, low, high)
         total = jnp.zeros((8, size), jnp.float32)
-        for start in range(0, whole, 8):
-            total += blocks_ref[e, start : start + 8, :] * columns[start : start + 8, e : e + 1]
+        for i in range(size // 8):
+            total += blocks_ref[e, 8 * i : 8 * i + 8, :] * element_in[:, i : i + 1]
         total = jnp.sum(total, axis=0, keepdims=True)
-        for line in range(whole, size):
-            total += blocks_ref[e, line : line + 1, :] * columns[line : line + 1, e : e + 1]
-        y_ref[e : e + 1, :size] = total
-    element_out = jnp.concatenate([y_ref[e : e + 1, :] for e in range(elements)], axis=1)
-    out_ref[:SUMS] = place(element_out, lane_ref[...], row_ref[...])
+        for i in range(size % 8):
+            value = element_in[i : i + 1, size // 8 : size // 8 + 1]
+            total += blocks_ref[e, whole + i : whole + i + 1, :] * value
+        row_hot = row_ref[:, e * width : e * width + size]
+        spread = half(jnp.concatenate([row_hot * part for part in split(total)], axis=0))
+        part = lax.dot_general(
+            spread,
+            lane_ref[:, e * width : e * width + size],
+            (((1,), (1,)), ((), ())),
+            preferred_element_type=jnp.float32,
+        )
+        sums = part if sums is None else sums + part
+    out_ref[:SUMS] = (sums[:SUMS] + sums[SUMS : 2 * SUMS]) + sums[2 * SUMS :]
     out_ref[SUMS:] = static_ref[...]
 
 
 def sum_kernel(count, *refs):
-    messages, (pair_lane_ref, pair_row_ref, own_ref, out_ref) = refs[:count], refs[count:]
+    messages, (own_ref, out_ref) = refs[:count], refs[count:]
     rows = own_ref.shape[0]
-    half_pairs = pair_lane_ref.shape[1] // 2
-    lines = half_pairs // LANES
-    lane_bits = LANES.bit_length() - 1
+    lines = (out_ref.shape[0] - TOTALS) // (5 * count)
     totals = [jnp.zeros((rows, LANES), jnp.float32) for _ in range(3)]
     old = jnp.zeros((1, LANES), jnp.float32)
     found = [[] for _ in range(5)]
@@ -194,18 +221,15 @@
         totals[1] += at(2) * applied
         totals[2] += at(0) * applied * applied
         base = SUMS + 24
+        if m == 0:
+            own_ref[...] = applied
+        low, high = lanes_of(message[base : base + 8].astype(jnp.int32))
+        values = look_up(applied, low, high)
+        found[0].append(values[:lines])
+        found[1].append(values[lines : 2 * lines])
+        base += 2 * lines
         old += message[base : base + 1]
         base += 1
-        if m == 0:
-            own_ref[...] = applied
-            pair_lane, pair_row = pair_lane_ref[...], pair_row_ref[...]
-        else:
-            slots = as_row(message[base + 3 * lines : base + 5 * lines]).astype(jnp.int32)
-            pair_lane = half(hot(jnp.where(slots < 0, -1, slots & (LANES - 1)), LANES))
-            pair_row = hot(lax.shift_right_arithmetic(slots, lane_bits), rows)
-        values = as_rows(pick(applied, pair_lane, pair_row))
-        found[0] += values[:lines]
-        found[1] += values[lines:]
         for i in range(3):
             found[2 + i].append(message[base + i * lines : base + (i + 1) * lines])
     heads = [old] + [jnp.sum(total, axis=0, keepdims=True) for total in totals]
@@ -227,8 +251,7 @@
     messages = [ref[...] for ref in refs[:count]]
     (
         own_ref,
-        pair_lane_ref,
-        pair_row_ref,
+        index_ref,
         vector_ref,
         new_solution_ref,
         new_residual_ref,
@@ -268,8 +291,11 @@
         terms[2] += part(near, 4) * backward * (2.0 * forward + backward)
         from_left = jnp.where(me == d + 1, forward[:lines], from_left)
         from_right = jnp.where(me == d, backward[:lines], from_right)
-    incoming = as_row(jnp.concatenate([from_right, from_left], axis=0))
-    applied = own_ref[...] + place(incoming, pair_lane_ref[...], pair_row_ref[...])
+    incoming = jnp.concatenate([from_right, from_left], axis=0)
+    last = index_ref.shape[0]
+    applied = own_ref[...] + look_up(
+        incoming, index_ref[last - 16 : last - 8], index_ref[last - 8 : last]
+    )
 
     def whole(value):
         return jnp.sum(value, axis=1, keepdims=True)
@@ -339,18 +365,17 @@
     first = lax.ppermute(direction, group, swap_first(group_count))
     second = lax.ppermute(direction, group, swap_second(group_count))
 
-    lane_hot, row_hot, pair_lane, pair_row, static, vectors = pl.pallas_call(
+    lane_hot, row_hot, index, static, vectors = pl.pallas_call(
         functools.partial(prepare_kernel, group),
         out_shape=[
             jax.ShapeDtypeStruct((LANES, elements * width), bf16),
             jax.ShapeDtypeStruct((3 * rows, elements * width), f32),
-            jax.ShapeDtypeStruct((LANES, 2 * pairs), bf16),
-            jax.ShapeDtypeStruct((rows, 2 * pairs), f32),
+            jax.ShapeDtypeStruct((16 * (elements + 1), LANES), jnp.int32),
             jax.ShapeDtypeStruct((STATIC, LANES), f32),
             jax.ShapeDtypeStruct((4 * rows, LANES), f32),
         ],
         in_specs=specs([pltpu.HBM] * 9),
-        out_specs=specs([vmem] * 6),
+        out_specs=specs([vmem] * 5),
         scratch_shapes=[
             pltpu.VMEM((elements, size), jnp.int32),
             pltpu.VMEM((8, width), jnp.int32),
@@ -383,12 +408,11 @@
     message = pl.pallas_call(
         element_kernel,
         out_shape=jax.ShapeDtypeStruct((SUMS + STATIC, LANES), f32),
-        in_specs=specs([vmem] * 7),
+        in_specs=specs([vmem] * 8),
         out_specs=pl.BlockSpec(memory_space=vmem),
-        scratch_shapes=[pltpu.VMEM((8, width), f32), pltpu.VMEM((8, width), f32)],
         compiler_params=params,
         name="elements",
-    )(vectors, first, second, schur_blocks, lane_hot, row_hot, static)
+    )(vectors, first, second, schur_blocks, lane_hot, row_hot, index, static)
 
     if group_count == 4:
         first = lax.ppermute(message, group, swap_first(group_count))
@@ -410,11 +434,11 @@
             jax.ShapeDtypeStruct((rows, LANES), f32),
             jax.ShapeDtypeStruct((TOTALS + 5 * group_count * lines, LANES), f32),
         ],
-        in_specs=specs([vmem] * (group_count + 2)),
+        in_specs=specs([vmem] * group_count),
         out_specs=specs([vmem] * 2),
         compiler_params=params,
         name="sums",
-    )(*messages, pair_lane, pair_row)
+    )(*messages)
 
     ordered = not (dom_count == 4 and sub_count == 2)
     if ordered:
@@ -432,11 +456,11 @@
     outputs = pl.pallas_call(
         functools.partial(final_kernel, dom, "sub", ordered, dom_count, lines),
         out_shape=[jax.ShapeDtypeStruct((rows, LANES), f32)] * 3,
-        in_specs=specs([vmem] * (dom_count + 4)),
+        in_specs=specs([vmem] * (dom_count + 3)),
         out_specs=specs([vmem] * 3),
         compiler_params=params,
         name="update",
-    )(*messages, own, pair_lane, pair_row, vectors)
+    )(*messages, own, index, vectors)
     return tuple(value.reshape(-1) for value in outputs)
 
 

time: 18.9 us -> 18.6 us (0.984)
  Pallas kernels: 3.44 us -> 3.21 us
    pallas_call x1, Pallas kernels: 1.17 us -> 0.98 us  [local(): pl.pallas_call(element_kernel, out_shape=jax.ShapeDtypeStruct((SUMS + STA...]
  transfers between devices with their start and end apart: 8 -> 8, of which waited for: 5 -> 5; matrix products, arithmetic and copies ran while one was open for 0% -> 0% of each run, Pallas kernels for 6% -> 7%
where the time goes in v5:
time: 18.6 us; the launch traced here: 18.4 us
  starting transfers between devices  9.58 us (52%)
  waiting for transfers between devices  4.94 us (27%)
  Pallas kernels  3.21 us (17%)
  between operations  0.67 us (4%)
    ppermute x1, starting transfers between devices, local(): direct = lax.ppermute(message, line, split)  3.71 us
    ppermute x1, starting transfers between devices, local(): second = lax.ppermute(direction, group, swap_second(group_count))  2.67 us
    ppermute x1, starting transfers between devices, local(): second = lax.ppermute(message, group, swap_second(group_count))  1.83 us
    ppermute x1, waiting for transfers between devices, local(): far = lax.ppermute(message, line, both)  1.83 us
    ppermute x1, waiting for transfers between devices, local(): second = lax.ppermute(message, group, swap_second(group_count))  1.49 us
    pallas_call x1, Pallas kernels, local(): pl.pallas_call(functools.partial(prepare_kernel, group), out_shape=[jax.S...  1.24 us
    pallas_call x1, Pallas kernels, local(): pl.pallas_call(element_kernel, out_shape=jax.ShapeDtypeStruct((SUMS + STA...  0.98 us
    ppermute x1, waiting for transfers between devices, local(): relayed = lax.ppermute(second, group, swap_first(group_count))  0.95 us
  transfers between devices with their start and end apart: 8, of which 5 were waited for; matrix products, arithmetic and copies ran while one was open for 0% of the time, Pallas kernels for 7%

profile of v5, /device:TPU:1, one launch (start us, length us, event | category | flops | bytes accessed | tf_op | source)
XLA Modules:
  0.0 18.4 jit_solution(2896983966200450571)
XLA Ops:
  0.6 0.0 copy-start
  0.6 2.7 %collective-permute-start.1 = (f32[8,128]{1,0:T(8,128)}, f32[8,128]{1,0:T(8,128)S(1)}, u32[]{:S(2)}, u32[]{:S(2)}) collective-permute-start(f32[8,128]{1,0:T(8,128)} %bitcast.10), channel_id=1, source_target_pairs={{0,3},{1,2},{2,1},{3,0},{4,7},{5,6},{6,5},{7,4},{8,11},{9,10},{10,... | collective-permute-start | bytes 12296 | tf_op jit(solution)/shard_map/ppermute | solution.py:366
  3.3 0.0 collective-permute-start
  3.3 1.2 %prepare.1 = (bf16[128,1920]{1,0:T(8,128)(2,1)S(1)}, f32[24,1920]{1,0:T(8,128)S(1)}, s32[64,128]{1,0:T(8,128)S(1)}, f32[40,128]{1,0:T(8,128)S(1)}, f32[32,128]{1,0:T(8,128)S(1)}) custom-call(s32[3]{0:T(128)} %order_hbm.1, s32[1,2]{1,0:T(1,128)} %count_hbm.1, s32[3,602]{1,0:T(4,128)} %dofs_hbm.1, s32[1,256]{1,0:T(1,128)} %left_hbm.1, s32[1,256]{1,0:T(1,128)} %right_hbm.1, ...), custom_call_target="tpu_custom_call" | custom-call | flops 1600000000 | bytes 16000000 | tf_op jit(solution)/shard_map/prepare/pallas_call | solution.py:368
  4.6 0.2 %collective-permute-done.1.second_ref = f32[8,128]{1,0:T(8,128)S(1)} collective-permute-done((f32[8,128]{1,0:T(8,128)}, f32[8,128]{1,0:T(8,128)S(1)}, u32[]{:S(2)}, u32[]{:S(2)}) %collective-permute-start.1) | collective-permute-done | bytes 4128 | tf_op jit(solution)/shard_map/ppermute | solution.py:366
  4.8 0.0 collective-permute-done.first_ref
  4.8 0.0 copy-done
  4.8 1.0 %elements.1.refs_0_ = f32[64,128]{1,0:T(8,128)S(1)} custom-call(f32[32,128]{1,0:T(8,128)S(1)} %get-tuple-element.13.vector_ref.refs_6_, f32[8,128]{1,0:T(8,128)S(1)} %collective-permute-done.first_ref, f32[8,128]{1,0:T(8,128)S(1)} %collective-permute-done.1.second_ref, f32[3,602,602]{2,1,0:T(8,128)S(1)} %copy-done, ...), custom_call_target="tpu_custom_call" | custom-call | tf_op jit(solution)/shard_map/elements/pallas_call | solution.py:408
  5.8 1.8 %collective-permute-start.3 = (f32[64,128]{1,0:T(8,128)S(1)}, f32[64,128]{1,0:T(8,128)S(1)}, u32[]{:S(2)}, u32[]{:S(2)}) collective-permute-start(f32[64,128]{1,0:T(8,128)S(1)} %elements.1.refs_0_), channel_id=1, source_target_pairs={{0,3},{1,2},{2,1},{3,0},{4,7},{5,6},{6,5},{7,4},{8,11},{9,10},{10,... | collective-permute-start | bytes 98312 | tf_op jit(solution)/shard_map/ppermute | solution.py:419
  7.6 0.1 collective-permute-start.2
  7.8 1.5 %collective-permute-done.3.refs_3_ = f32[64,128]{1,0:T(8,128)S(1)} collective-permute-done((f32[64,128]{1,0:T(8,128)S(1)}, f32[64,128]{1,0:T(8,128)S(1)}, u32[]{:S(2)}, u32[]{:S(2)}) %collective-permute-start.3) | collective-permute-done | bytes 32800 | tf_op jit(solution)/shard_map/ppermute | solution.py:419
  9.2 0.3 %collective-permute-start.4 = (f32[64,128]{1,0:T(8,128)S(1)}, f32[64,128]{1,0:T(8,128)S(1)}, u32[]{:S(2)}, u32[]{:S(2)}) collective-permute-start(f32[64,128]{1,0:T(8,128)S(1)} %collective-permute-done.3.refs_3_), channel_id=1, source_target_pairs={{0,1},{1,0},{2,3},{3,2},{4,5},{5,4},{6,7},{7,6},{8,9},{9,8},{10,11... | collective-permute-start | bytes 98312 | tf_op jit(solution)/shard_map/ppermute | solution.py:420
  9.5 0.0 collective-permute-done.2.refs_1_
  9.5 0.9 %collective-permute-done.4.refs_2_ = f32[64,128]{1,0:T(8,128)S(1)} collective-permute-done((f32[64,128]{1,0:T(8,128)S(1)}, f32[64,128]{1,0:T(8,128)S(1)}, u32[]{:S(2)}, u32[]{:S(2)}) %collective-permute-start.4) | collective-permute-done | bytes 32800 | tf_op jit(solution)/shard_map/ppermute | solution.py:420
  10.4 0.1 sums.1
  10.6 3.7 %collective-permute-start.5 = (f32[48,128]{1,0:T(8,128)S(1)}, f32[48,128]{1,0:T(8,128)S(1)}, u32[]{:S(2)}, u32[]{:S(2)}) collective-permute-start(f32[48,128]{1,0:T(8,128)S(1)} %get-tuple-element.18.refs_0_), channel_id=1, source_target_pairs={{0,8},{1,13},{4,12},{5,9},{8,0},{9,5},{12,4},{13,1},{2,10},{3,15},... | collective-permute-start | bytes 73736 | tf_op jit(solution)/shard_map/ppermute | solution.py:451
  14.3 0.8 %collective-permute-start.6 = (f32[48,128]{1,0:T(8,128)S(1)}, f32[48,128]{1,0:T(8,128)S(1)}, u32[]{:S(2)}, u32[]{:S(2)}) collective-permute-start(f32[48,128]{1,0:T(8,128)S(1)} %get-tuple-element.18.refs_0_), channel_id=1, source_target_pairs={{0,5},{1,4},{4,1},{5,0},{8,13},{9,12},{12,9},{13,8},{2,7},{3,6},{6... | collective-permute-start | bytes 73736 | tf_op jit(solution)/shard_map/ppermute | solution.py:452
  15.1 0.4 %collective-permute-done.5.refs_1_ = f32[48,128]{1,0:T(8,128)S(1)} collective-permute-done((f32[48,128]{1,0:T(8,128)S(1)}, f32[48,128]{1,0:T(8,128)S(1)}, u32[]{:S(2)}, u32[]{:S(2)}) %collective-permute-start.5) | collective-permute-done | bytes 24608 | tf_op jit(solution)/shard_map/ppermute | solution.py:451
  15.5 0.2 %collective-permute-start.7 = (f32[48,128]{1,0:T(8,128)S(1)}, f32[48,128]{1,0:T(8,128)S(1)}, u32[]{:S(2)}, u32[]{:S(2)}) collective-permute-start(f32[48,128]{1,0:T(8,128)S(1)} %collective-permute-done.5.refs_1_), channel_id=1, source_target_pairs={{0,1},{1,0},{2,3},{3,2},{4,5},{5,4},{6,7},{7,6},{8,9},{9,8},{10,11... | collective-permute-start | bytes 73736 | tf_op jit(solution)/shard_map/ppermute | solution.py:453
  15.7 1.8 %collective-permute-done.6.refs_2_ = f32[48,128]{1,0:T(8,128)S(1)} collective-permute-done((f32[48,128]{1,0:T(8,128)S(1)}, f32[48,128]{1,0:T(8,128)S(1)}, u32[]{:S(2)}, u32[]{:S(2)}) %collective-permute-start.6) | collective-permute-done | bytes 24608 | tf_op jit(solution)/shard_map/ppermute | solution.py:452
  17.5 0.0 collective-permute-done.7.refs_3_
  17.5 0.9 %update.1 = (f32[8,128]{1,0:T(8,128)}, f32[8,128]{1,0:T(8,128)}, f32[8,128]{1,0:T(8,128)}) custom-call(f32[48,128]{1,0:T(8,128)S(1)} %get-tuple-element.18.refs_0_, f32[48,128]{1,0:T(8,128)S(1)} %collective-permute-done.5.refs_1_, f32[48,128]{1,0:T(8,128)S(1)} %collective-permute-done.6.refs_2_, f32[48,128]{1,0:T(8,128)S(1)} %collective-permute-done.7.refs_3_, ...), custom_call_target="tpu_custom_call" | custom-call | tf_op jit(solution)/shard_map/update/pallas_call | solution.py:456
Async XLA Ops:
  0.6 4.2 %copy-start = (f32[3,602,602]{2,1,0:T(8,128)S(1)}, f32[3,602,602]{2,1,0:T(8,128)}, u32[]{:S(2)}) copy-start(f32[3,602,602]{2,1,0:T(8,128)} %blocks_ref.1) | copy-start | bytes 13046548
  0.6 4.2 %collective-permute-start.1 = (f32[8,128]{1,0:T(8,128)}, f32[8,128]{1,0:T(8,128)S(1)}, u32[]{:S(2)}, u32[]{:S(2)}) collective-permute-start(f32[8,128]{1,0:T(8,128)} %bitcast.10), channel_id=1, source_target_pairs={{0,3},{1,2},{2,1},{3,0},{4,7},{5,6},{6,5},{7,4},{8,11},{9,10},{10,... | collective-permute-start | bytes 12296 | tf_op jit(solution)/shard_map/ppermute | solution.py:366
  3.3 1.5 %collective-permute-start = (f32[8,128]{1,0:T(8,128)}, f32[8,128]{1,0:T(8,128)S(1)}, u32[]{:S(2)}, u32[]{:S(2)}) collective-permute-start(f32[8,128]{1,0:T(8,128)} %bitcast.11), channel_id=1, source_target_pairs={{0,1},{1,0},{2,3},{3,2},{4,5},{5,4},{6,7},{7,6},{8,9},{9,8},{10,11... | collective-permute-start | bytes 12296 | tf_op jit(solution)/shard_map/ppermute | solution.py:365
  5.8 3.4 %collective-permute-start.3 = (f32[64,128]{1,0:T(8,128)S(1)}, f32[64,128]{1,0:T(8,128)S(1)}, u32[]{:S(2)}, u32[]{:S(2)}) collective-permute-start(f32[64,128]{1,0:T(8,128)S(1)} %elements.1.refs_0_), channel_id=1, source_target_pairs={{0,3},{1,2},{2,1},{3,0},{4,7},{5,6},{6,5},{7,4},{8,11},{9,10},{10,... | collective-permute-start | bytes 98312 | tf_op jit(solution)/shard_map/ppermute | solution.py:419
  7.6 1.9 %collective-permute-start.2 = (f32[64,128]{1,0:T(8,128)S(1)}, f32[64,128]{1,0:T(8,128)S(1)}, u32[]{:S(2)}, u32[]{:S(2)}) collective-permute-start(f32[64,128]{1,0:T(8,128)S(1)} %elements.1.refs_0_), channel_id=1, source_target_pairs={{0,1},{1,0},{2,3},{3,2},{4,5},{5,4},{6,7},{7,6},{8,9},{9,8},{10,11... | collective-permute-start | bytes 98312 | tf_op jit(solution)/shard_map/ppermute | solution.py:418
  9.2 1.2 %collective-permute-start.4 = (f32[64,128]{1,0:T(8,128)S(1)}, f32[64,128]{1,0:T(8,128)S(1)}, u32[]{:S(2)}, u32[]{:S(2)}) collective-permute-start(f32[64,128]{1,0:T(8,128)S(1)} %collective-permute-done.3.refs_3_), channel_id=1, source_target_pairs={{0,1},{1,0},{2,3},{3,2},{4,5},{5,4},{6,7},{7,6},{8,9},{9,8},{10,11... | collective-permute-start | bytes 98312 | tf_op jit(solution)/shard_map/ppermute | solution.py:420
  10.6 4.9 %collective-permute-start.5 = (f32[48,128]{1,0:T(8,128)S(1)}, f32[48,128]{1,0:T(8,128)S(1)}, u32[]{:S(2)}, u32[]{:S(2)}) collective-permute-start(f32[48,128]{1,0:T(8,128)S(1)} %get-tuple-element.18.refs_0_), channel_id=1, source_target_pairs={{0,8},{1,13},{4,12},{5,9},{8,0},{9,5},{12,4},{13,1},{2,10},{3,15},... | collective-permute-start | bytes 73736 | tf_op jit(solution)/shard_map/ppermute | solution.py:451
  14.3 3.3 %collective-permute-start.6 = (f32[48,128]{1,0:T(8,128)S(1)}, f32[48,128]{1,0:T(8,128)S(1)}, u32[]{:S(2)}, u32[]{:S(2)}) collective-permute-start(f32[48,128]{1,0:T(8,128)S(1)} %get-tuple-element.18.refs_0_), channel_id=1, source_target_pairs={{0,5},{1,4},{4,1},{5,0},{8,13},{9,12},{12,9},{13,8},{2,7},{3,6},{6... | collective-permute-start | bytes 73736 | tf_op jit(solution)/shard_map/ppermute | solution.py:452
  15.5 2.0 %collective-permute-start.7 = (f32[48,128]{1,0:T(8,128)S(1)}, f32[48,128]{1,0:T(8,128)S(1)}, u32[]{:S(2)}, u32[]{:S(2)}) collective-permute-start(f32[48,128]{1,0:T(8,128)S(1)} %collective-permute-done.5.refs_1_), channel_id=1, source_target_pairs={{0,1},{1,0},{2,3},{3,2},{4,5},{5,4},{6,7},{7,6},{8,9},{9,8},{10,11... | collective-permute-start | bytes 73736 | tf_op jit(solution)/shard_map/ppermute | solution.py:453

commit v6 on v5

--- a/solution.py
+++ b/solution.py
@@ -27,13 +27,19 @@
     return value.astype(jnp.bfloat16)
 
 
-def look_up(table, low, high):
-    found = jnp.zeros(low.shape, jnp.float32)
+def look_up(table, low, high, found=None):
+    if found is None:
+        found = jnp.zeros(low.shape, jnp.float32)
     for row in range(table.shape[0]):
         line = jnp.broadcast_to(table[row : row + 1], low.shape)
         line = jnp.take_along_axis(line, low, axis=1, mode="promise_in_bounds")
         found = jnp.where(high == row, line, found)
     return found
+
+
+def spread_lane(value, lane):
+    index = jnp.full(value.shape, lane, jnp.int32)
+    return jnp.take_along_axis(value, index, axis=1, mode="promise_in_bounds")
 
 
 def lanes_of(slots):
@@ -72,6 +78,7 @@
     lane_ref,
     row_ref,
     index_ref,
+    in_ref,
     static_ref,
     vector_ref,
     dofs_ref,
@@ -133,10 +140,18 @@
     packed = jnp.dot(
         half(jnp.concatenate(parts, axis=0)), half(tile), preferred_element_type=jnp.float32
     )
-    packed = packed.astype(jnp.int32) - 1
-    for e in range(elements):
-        index_ref[16 * e : 16 * e + 8] = jnp.maximum(packed[16 * e : 16 * e + 8], 0)
-        index_ref[16 * e + 8 : 16 * e + 16] = packed[16 * e + 8 : 16 * e + 16]
+    tiles = -(-size // 8)
+    packed = [packed[16 * e : 16 * e + 16, :tiles] for e in range(elements)]
+    registers = in_ref.shape[0] // 8
+    packed.append(jnp.zeros((16, registers * LANES - elements * tiles), jnp.float32))
+    packed = jnp.concatenate(packed, axis=1).astype(jnp.int32) - 1
+    direction = vector_ref[2 * rows : 3 * rows]
+    for i in range(registers):
+        register = packed[:, i * LANES : (i + 1) * LANES]
+        low, high = jnp.maximum(register[:8], 0), register[8:]
+        index_ref[16 * i : 16 * i + 8] = low
+        index_ref[16 * i + 8 : 16 * i + 16] = high - rows
+        in_ref[8 * i : 8 * i + 8] = look_up(direction, low, high)
     pairs = left_ref.shape[1]
     pair_lanes = lax.broadcasted_iota(jnp.int32, (1, pairs), 1)
     right = jnp.where(pair_lanes < count_ref[0, 1], right_ref[...], -1)
@@ -151,11 +166,10 @@
     )
     source = source.astype(jnp.int32) - 1
     low, high = lanes_of(source)
-    index_ref[16 * elements : 16 * elements + 8] = low
-    index_ref[16 * elements + 8 : 16 * elements + 16] = high
+    index_ref[16 * registers : 16 * registers + 8] = low
+    index_ref[16 * registers + 8 : 16 * registers + 16] = high
     owner = jnp.where(source >= pairs, 0.0, 1.0)
     residual = vector_ref[rows : 2 * rows]
-    direction = vector_ref[2 * rows : 3 * rows]
     diagonal = vector_ref[3 * rows : 4 * rows]
     scaled = diagonal * residual
     static_ref[0:8] = owner * diagonal
@@ -174,26 +188,34 @@
 
 
 def element_kernel(
-    vector_ref, first_ref, second_ref, blocks_ref, lane_ref, row_ref, index_ref, static_ref, out_ref
+    first_ref, second_ref, blocks_ref, lane_ref, row_ref, index_ref, in_ref, static_ref, out_ref
 ):
     elements, size, _ = blocks_ref.shape
     width = lane_ref.shape[1] // elements
-    rows = first_ref.shape[0]
-    window = jnp.concatenate(
-        [vector_ref[2 * rows : 3 * rows], first_ref[...], second_ref[...]], axis=0
-    )
+    tiles = -(-size // 8)
     whole = size // 8 * 8
+    window = jnp.concatenate([first_ref[...], second_ref[...]], axis=0)
+    element_in = [
+        look_up(
+            window,
+            index_ref[16 * i : 16 * i + 8],
+            index_ref[16 * i + 8 : 16 * i + 16],
+            in_ref[8 * i : 8 * i + 8],
+        )
+        for i in range(in_ref.shape[0] // 8)
+    ]
     sums = None
     for e in range(elements):
-        low, high = index_ref[16 * e : 16 * e + 8], index_ref[16 * e + 8 : 16 * e + 16]
-        element_in = look_up(window, low, high)
         total = jnp.zeros((8, size), jnp.float32)
-        for i in range(size // 8):
-            total += blocks_ref[e, 8 * i : 8 * i + 8, :] * element_in[:, i : i + 1]
+        for i in range(tiles):
+            column = e * tiles + i
+            value = spread_lane(element_in[column // LANES], column % LANES)
+            value = jnp.concatenate([value] * (width // LANES), axis=1)[:, :size]
+            if 8 * i < whole:
+                total += blocks_ref[e, 8 * i : 8 * i + 8, :] * value
         total = jnp.sum(total, axis=0, keepdims=True)
         for i in range(size % 8):
-            value = element_in[i : i + 1, size // 8 : size // 8 + 1]
-            total += blocks_ref[e, whole + i : whole + i + 1, :] * value
+            total += blocks_ref[e, whole + i : whole + i + 1, :] * value[i : i + 1]
         row_hot = row_ref[:, e * width : e * width + size]
         spread = half(jnp.concatenate([row_hot * part for part in split(total)], axis=0))
         part = lax.dot_general(
@@ -260,13 +282,13 @@
     rows = own_ref.shape[0]
     me = lax.axis_index(dom_axis)
     if not ordered:
-        own, direct, far, relayed = messages
-        far, relayed = (other_order(value, TOTALS, lines) for value in (far, relayed))
+        own, direct, near, relayed = messages
+        direct = other_order(direct, TOTALS, lines)
         even = lax.axis_index(inner_axis) == 0
         line = [own] + [None] * 3
-        line[SPLIT[0]] = jnp.where(even, direct, relayed)
-        line[SPLIT[1]] = jnp.where(even, relayed, direct)
-        line[BOTH] = far
+        line[SPLIT[0]] = jnp.where(even, relayed, direct)
+        line[SPLIT[1]] = jnp.where(even, direct, relayed)
+        line[BOTH] = near
         low = (me & 1) == 0
         high = (me & 2) == 0
         line = [jnp.where(low, line[i], line[i ^ 1]) for i in range(4)]
@@ -365,17 +387,19 @@
     first = lax.ppermute(direction, group, swap_first(group_count))
     second = lax.ppermute(direction, group, swap_second(group_count))
 
-    lane_hot, row_hot, index, static, vectors = pl.pallas_call(
+    registers = -(-elements * -(-size // 8) // LANES)
+    lane_hot, row_hot, index, element_in, static, vectors = pl.pallas_call(
         functools.partial(prepare_kernel, group),
         out_shape=[
             jax.ShapeDtypeStruct((LANES, elements * width), bf16),
             jax.ShapeDtypeStruct((3 * rows, elements * width), f32),
-            jax.ShapeDtypeStruct((16 * (elements + 1), LANES), jnp.int32),
+            jax.ShapeDtypeStruct((16 * (registers + 1), LANES), jnp.int32),
+            jax.ShapeDtypeStruct((8 * registers, LANES), f32),
             jax.ShapeDtypeStruct((STATIC, LANES), f32),
             jax.ShapeDtypeStruct((4 * rows, LANES), f32),
         ],
         in_specs=specs([pltpu.HBM] * 9),
-        out_specs=specs([vmem] * 5),
+        out_specs=specs([vmem] * 6),
         scratch_shapes=[
             pltpu.VMEM((elements, size), jnp.int32),
             pltpu.VMEM((8, width), jnp.int32),
@@ -412,7 +436,7 @@
         out_specs=pl.BlockSpec(memory_space=vmem),
         compiler_params=params,
         name="elements",
-    )(vectors, first, second, schur_blocks, lane_hot, row_hot, index, static)
+    )(first, second, schur_blocks, lane_hot, row_hot, index, element_in, static)
 
     if group_count == 4:
         first = lax.ppermute(message, group, swap_first(group_count))
@@ -446,12 +470,12 @@
         messages = [everyone[d] for d in range(dom_count)]
     else:
         line = (dom, "sub")
-        split = [(2 * d + s, 2 * (d ^ SPLIT[s]) + s) for d in range(4) for s in range(2)]
-        both = [(2 * d + s, 2 * (d ^ BOTH) + 1 - s) for d in range(4) for s in range(2)]
+        split = [(2 * d + s, 2 * (d ^ SPLIT[s]) + 1 - s) for d in range(4) for s in range(2)]
+        both = [(2 * d + s, 2 * (d ^ BOTH) + s) for d in range(4) for s in range(2)]
         direct = lax.ppermute(message, line, split)
-        far = lax.ppermute(message, line, both)
+        near = lax.ppermute(message, line, both)
         relayed = lax.ppermute(direct, "sub", [(0, 1), (1, 0)])
-        messages = [message, direct, far, relayed]
+        messages = [message, direct, near, relayed]
 
     outputs = pl.pallas_call(
         functools.partial(final_kernel, dom, "sub", ordered, dom_count, lines),

time: 18.6 us -> 18.3 us (0.984)
  the two profiles are of different devices: /device:TPU:1 before, /device:TPU:0 now
where the time goes in v6:
time: 18.3 us; the launch traced here: 18.1 us
  starting transfers between devices  9.51 us (52%)
  waiting for transfers between devices  4.77 us (26%)
  Pallas kernels  3.17 us (17%)
  between operations  0.69 us (4%)
    ppermute x1, starting transfers between devices, local(): direct = lax.ppermute(message, line, split)  2.7 us
    ppermute x1, starting transfers between devices, local(): second = lax.ppermute(direction, group, swap_second(group_count))  2.44 us
    ppermute x1, starting transfers between devices, local(): near = lax.ppermute(message, line, both)  1.58 us
    ppermute x1, starting transfers between devices, local(): second = lax.ppermute(message, group, swap_second(group_count))  1.56 us
    ppermute x1, waiting for transfers between devices, local(): second = lax.ppermute(message, group, swap_second(group_count))  1.47 us
    pallas_call x1, Pallas kernels, local(): pl.pallas_call(functools.partial(prepare_kernel, group), out_shape=[jax.S...  1.35 us
    ppermute x1, waiting for transfers between devices, local(): near = lax.ppermute(message, line, both)  1.29 us
    ppermute x1, waiting for transfers between devices, local(): relayed = lax.ppermute(second, group, swap_first(group_count))  1.05 us
  transfers between devices with their start and end apart: 8, of which 4 were waited for; matrix products, arithmetic and copies ran while one was open for 0% of the time, Pallas kernels for 7%

profile of v6, /device:TPU:0, one launch (start us, length us, event | category | flops | bytes accessed | tf_op | source)
XLA Modules:
  0.0 18.1 jit_solution(8436317422336901511)
XLA Ops:
  0.6 0.0 copy-start
  0.6 2.4 %collective-permute-start.1 = (f32[8,128]{1,0:T(8,128)}, f32[8,128]{1,0:T(8,128)S(1)}, u32[]{:S(2)}, u32[]{:S(2)}) collective-permute-start(f32[8,128]{1,0:T(8,128)} %bitcast.10), channel_id=1, source_target_pairs={{0,3},{1,2},{2,1},{3,0},{4,7},{5,6},{6,5},{7,4},{8,11},{9,10},{10,... | collective-permute-start | bytes 12296 | tf_op jit(solution)/shard_map/ppermute | solution.py:388
  3.1 0.7 %collective-permute-start = (f32[8,128]{1,0:T(8,128)}, f32[8,128]{1,0:T(8,128)S(1)}, u32[]{:S(2)}, u32[]{:S(2)}) collective-permute-start(f32[8,128]{1,0:T(8,128)} %bitcast.11), channel_id=1, source_target_pairs={{0,1},{1,0},{2,3},{3,2},{4,5},{5,4},{6,7},{7,6},{8,9},{9,8},{10,11... | collective-permute-start | bytes 12296 | tf_op jit(solution)/shard_map/ppermute | solution.py:387
  3.8 1.4 %prepare.1 = (bf16[128,1920]{1,0:T(8,128)(2,1)S(1)}, f32[24,1920]{1,0:T(8,128)S(1)}, s32[48,128]{1,0:T(8,128)S(1)}, f32[16,128]{1,0:T(8,128)S(1)}, f32[40,128]{1,0:T(8,128)S(1)}, /*index=5*/f32[32,128]{1,0:T(8,128)S(1)}) custom-call(s32[3]{0:T(128)} %order_hbm.1, s32[1,2]{1,0:T(1,128)} %count_hbm.1, s32[3,602]{1,0:T(4,128)} %dofs_hbm.1, s32[1,256]{1,0:T(1,128)} %left_hbm.1, ...), custom_call_target="tpu_custom_call" | custom-call | flops 1600000000 | bytes 16000000 | tf_op jit(solution)/shard_map/prepare/pallas_call | solution.py:391
  5.1 0.0 collective-permute-done.1.second_ref
  5.1 0.0 collective-permute-done.first_ref
  5.1 0.0 copy-done
  5.2 0.8 %elements.1.refs_0_ = f32[64,128]{1,0:T(8,128)S(1)} custom-call(f32[8,128]{1,0:T(8,128)S(1)} %collective-permute-done.first_ref, f32[8,128]{1,0:T(8,128)S(1)} %collective-permute-done.1.second_ref, f32[3,602,602]{2,1,0:T(8,128)S(1)} %copy-done, bf16[128,1920]{1,0:T(8,128)(2,1)S(1)} %get-tuple-element.14.lane_ref, f32[24,1920]{1,0:T(8,128)S(1)} %get-tuple-element.15.row_ref, ...), custom_call_target="tpu_custom_call" | custom-call | tf_op jit(solution)/shard_map/elements/pallas_call | solution.py:432
  6.0 1.6 %collective-permute-start.3 = (f32[64,128]{1,0:T(8,128)S(1)}, f32[64,128]{1,0:T(8,128)S(1)}, u32[]{:S(2)}, u32[]{:S(2)}) collective-permute-start(f32[64,128]{1,0:T(8,128)S(1)} %elements.1.refs_0_), channel_id=1, source_target_pairs={{0,3},{1,2},{2,1},{3,0},{4,7},{5,6},{6,5},{7,4},{8,11},{9,10},{10,... | collective-permute-start | bytes 98312 | tf_op jit(solution)/shard_map/ppermute | solution.py:443
  7.5 0.4 %collective-permute-start.2 = (f32[64,128]{1,0:T(8,128)S(1)}, f32[64,128]{1,0:T(8,128)S(1)}, u32[]{:S(2)}, u32[]{:S(2)}) collective-permute-start(f32[64,128]{1,0:T(8,128)S(1)} %elements.1.refs_0_), channel_id=1, source_target_pairs={{0,1},{1,0},{2,3},{3,2},{4,5},{5,4},{6,7},{7,6},{8,9},{9,8},{10,11... | collective-permute-start | bytes 98312 | tf_op jit(solution)/shard_map/ppermute | solution.py:442
  7.9 1.5 %collective-permute-done.3.refs_3_ = f32[64,128]{1,0:T(8,128)S(1)} collective-permute-done((f32[64,128]{1,0:T(8,128)S(1)}, f32[64,128]{1,0:T(8,128)S(1)}, u32[]{:S(2)}, u32[]{:S(2)}) %collective-permute-start.3) | collective-permute-done | bytes 32800 | tf_op jit(solution)/shard_map/ppermute | solution.py:443
  9.4 0.2 collective-permute-start.4
  9.6 0.0 collective-permute-done.2.refs_1_
  9.6 1.0 %collective-permute-done.4.refs_2_ = f32[64,128]{1,0:T(8,128)S(1)} collective-permute-done((f32[64,128]{1,0:T(8,128)S(1)}, f32[64,128]{1,0:T(8,128)S(1)}, u32[]{:S(2)}, u32[]{:S(2)}) %collective-permute-start.4) | collective-permute-done | bytes 32800 | tf_op jit(solution)/shard_map/ppermute | solution.py:444
  10.6 0.1 sums.1
  10.7 2.7 %collective-permute-start.5 = (f32[48,128]{1,0:T(8,128)S(1)}, f32[48,128]{1,0:T(8,128)S(1)}, u32[]{:S(2)}, u32[]{:S(2)}) collective-permute-start(f32[48,128]{1,0:T(8,128)S(1)} %get-tuple-element.19.refs_0_), channel_id=1, source_target_pairs={{0,9},{1,12},{4,13},{5,8},{8,1},{9,4},{12,5},{13,0},{2,11},{3,14},... | collective-permute-start | bytes 73736 | tf_op jit(solution)/shard_map/ppermute | solution.py:475
  13.4 1.6 %collective-permute-start.6 = (f32[48,128]{1,0:T(8,128)S(1)}, f32[48,128]{1,0:T(8,128)S(1)}, u32[]{:S(2)}, u32[]{:S(2)}) collective-permute-start(f32[48,128]{1,0:T(8,128)S(1)} %get-tuple-element.19.refs_0_), channel_id=1, source_target_pairs={{0,4},{1,5},{4,0},{5,1},{8,12},{9,13},{12,8},{13,9},{2,6},{3,7},{6... | collective-permute-start | bytes 73736 | tf_op jit(solution)/shard_map/ppermute | solution.py:476
  15.0 0.9 %collective-permute-done.5.refs_1_ = f32[48,128]{1,0:T(8,128)S(1)} collective-permute-done((f32[48,128]{1,0:T(8,128)S(1)}, f32[48,128]{1,0:T(8,128)S(1)}, u32[]{:S(2)}, u32[]{:S(2)}) %collective-permute-start.5) | collective-permute-done | bytes 24608 | tf_op jit(solution)/shard_map/ppermute | solution.py:475
  16.0 0.0 collective-permute-start.7
  16.0 1.3 %collective-permute-done.6.refs_2_ = f32[48,128]{1,0:T(8,128)S(1)} collective-permute-done((f32[48,128]{1,0:T(8,128)S(1)}, f32[48,128]{1,0:T(8,128)S(1)}, u32[]{:S(2)}, u32[]{:S(2)}) %collective-permute-start.6) | collective-permute-done | bytes 24608 | tf_op jit(solution)/shard_map/ppermute | solution.py:476
  17.3 0.0 collective-permute-done.7.refs_3_
  17.3 0.9 %update.1 = (f32[8,128]{1,0:T(8,128)}, f32[8,128]{1,0:T(8,128)}, f32[8,128]{1,0:T(8,128)}) custom-call(f32[48,128]{1,0:T(8,128)S(1)} %get-tuple-element.19.refs_0_, f32[48,128]{1,0:T(8,128)S(1)} %collective-permute-done.5.refs_1_, f32[48,128]{1,0:T(8,128)S(1)} %collective-permute-done.6.refs_2_, f32[48,128]{1,0:T(8,128)S(1)} %collective-permute-done.7.refs_3_, ...), custom_call_target="tpu_custom_call" | custom-call | tf_op jit(solution)/shard_map/update/pallas_call | solution.py:480
Async XLA Ops:
  0.6 4.5 %copy-start = (f32[3,602,602]{2,1,0:T(8,128)S(1)}, f32[3,602,602]{2,1,0:T(8,128)}, u32[]{:S(2)}) copy-start(f32[3,602,602]{2,1,0:T(8,128)} %blocks_ref.1) | copy-start | bytes 13046548
  0.6 4.5 %collective-permute-start.1 = (f32[8,128]{1,0:T(8,128)}, f32[8,128]{1,0:T(8,128)S(1)}, u32[]{:S(2)}, u32[]{:S(2)}) collective-permute-start(f32[8,128]{1,0:T(8,128)} %bitcast.10), channel_id=1, source_target_pairs={{0,3},{1,2},{2,1},{3,0},{4,7},{5,6},{6,5},{7,4},{8,11},{9,10},{10,... | collective-permute-start | bytes 12296 | tf_op jit(solution)/shard_map/ppermute | solution.py:388
  3.1 2.0 %collective-permute-start = (f32[8,128]{1,0:T(8,128)}, f32[8,128]{1,0:T(8,128)S(1)}, u32[]{:S(2)}, u32[]{:S(2)}) collective-permute-start(f32[8,128]{1,0:T(8,128)} %bitcast.11), channel_id=1, source_target_pairs={{0,1},{1,0},{2,3},{3,2},{4,5},{5,4},{6,7},{7,6},{8,9},{9,8},{10,11... | collective-permute-start | bytes 12296 | tf_op jit(solution)/shard_map/ppermute | solution.py:387
  6.0 3.4 %collective-permute-start.3 = (f32[64,128]{1,0:T(8,128)S(1)}, f32[64,128]{1,0:T(8,128)S(1)}, u32[]{:S(2)}, u32[]{:S(2)}) collective-permute-start(f32[64,128]{1,0:T(8,128)S(1)} %elements.1.refs_0_), channel_id=1, source_target_pairs={{0,3},{1,2},{2,1},{3,0},{4,7},{5,6},{6,5},{7,4},{8,11},{9,10},{10,... | collective-permute-start | bytes 98312 | tf_op jit(solution)/shard_map/ppermute | solution.py:443
  7.5 2.0 %collective-permute-start.2 = (f32[64,128]{1,0:T(8,128)S(1)}, f32[64,128]{1,0:T(8,128)S(1)}, u32[]{:S(2)}, u32[]{:S(2)}) collective-permute-start(f32[64,128]{1,0:T(8,128)S(1)} %elements.1.refs_0_), channel_id=1, source_target_pairs={{0,1},{1,0},{2,3},{3,2},{4,5},{5,4},{6,7},{7,6},{8,9},{9,8},{10,11... | collective-permute-start | bytes 98312 | tf_op jit(solution)/shard_map/ppermute | solution.py:442
  9.4 1.2 %collective-permute-start.4 = (f32[64,128]{1,0:T(8,128)S(1)}, f32[64,128]{1,0:T(8,128)S(1)}, u32[]{:S(2)}, u32[]{:S(2)}) collective-permute-start(f32[64,128]{1,0:T(8,128)S(1)} %collective-permute-done.3.refs_3_), channel_id=1, source_target_pairs={{0,1},{1,0},{2,3},{3,2},{4,5},{5,4},{6,7},{7,6},{8,9},{9,8},{10,11... | collective-permute-start | bytes 98312 | tf_op jit(solution)/shard_map/ppermute | solution.py:444
  10.7 5.2 %collective-permute-start.5 = (f32[48,128]{1,0:T(8,128)S(1)}, f32[48,128]{1,0:T(8,128)S(1)}, u32[]{:S(2)}, u32[]{:S(2)}) collective-permute-start(f32[48,128]{1,0:T(8,128)S(1)} %get-tuple-element.19.refs_0_), channel_id=1, source_target_pairs={{0,9},{1,12},{4,13},{5,8},{8,1},{9,4},{12,5},{13,0},{2,11},{3,14},... | collective-permute-start | bytes 73736 | tf_op jit(solution)/shard_map/ppermute | solution.py:475
  13.4 3.8 %collective-permute-start.6 = (f32[48,128]{1,0:T(8,128)S(1)}, f32[48,128]{1,0:T(8,128)S(1)}, u32[]{:S(2)}, u32[]{:S(2)}) collective-permute-start(f32[48,128]{1,0:T(8,128)S(1)} %get-tuple-element.19.refs_0_), channel_id=1, source_target_pairs={{0,4},{1,5},{4,0},{5,1},{8,12},{9,13},{12,8},{13,9},{2,6},{3,7},{6... | collective-permute-start | bytes 73736 | tf_op jit(solution)/shard_map/ppermute | solution.py:476
  16.0 1.3 %collective-permute-start.7 = (f32[48,128]{1,0:T(8,128)S(1)}, f32[48,128]{1,0:T(8,128)S(1)}, u32[]{:S(2)}, u32[]{:S(2)}) collective-permute-start(f32[48,128]{1,0:T(8,128)S(1)} %collective-permute-done.5.refs_1_), channel_id=1, source_target_pairs={{0,1},{1,0},{2,3},{3,2},{4,5},{5,4},{6,7},{7,6},{8,9},{9,8},{10,11... | collective-permute-start | bytes 73736 | tf_op jit(solution)/shard_map/ppermute | solution.py:477
